TPU v7x, 32 devices: a whole 2x2x4 slice. The times are simulated.
32 devices in a mesh: shard: 8 (over z, x), ctx: 2 (over y), tp: 2 (over core).
Axes of the slice: x: 2, y: 2, z: 4, core: 2. Of those that a mesh axis runs over, the one named last changes fastest.
Arguments:
- inputs: bfloat16 [16384, 1024], P(('shard', 'ctx')), may hold values from -6 to 6
- cotangent: bfloat16 [16384, 1024], P(('shard', 'ctx')), may hold values from -8 to 8
- w_qkv: float32 [3, 1024, 1024], P(None, 'shard', 'tp'), may hold values from -0.25 to 0.25
- m_qkv: float32 [3, 1024, 1024], P(None, 'shard', 'tp'), may hold values from -80 to 80
- v_qkv: float32 [3, 1024, 1024], P(None, 'shard', 'tp'), may hold values from 491.52 to 6553.6
- w_dense: float32 [1024, 1024], P('tp', 'shard'), may hold values from -0.75 to 0.75
- m_dense: float32 [1024, 1024], P('tp', 'shard'), may hold values from -28 to 28
- v_dense: float32 [1024, 1024], P('tp', 'shard'), may hold values from 49.152 to 655.36
- w_fc1: float32 [1024, 4096], P('shard', 'tp'), may hold values from -0.1875 to 0.1875
- m_fc1: float32 [1024, 4096], P('shard', 'tp'), may hold values from -28 to 28
- v_fc1: float32 [1024, 4096], P('shard', 'tp'), may hold values from 49.152 to 655.36
- w_fc2: float32 [4096, 1024], P('tp', 'shard'), may hold values from -0.09375 to 0.09375
- m_fc2: float32 [4096, 1024], P('tp', 'shard'), may hold values from -56 to 56
- v_fc2: float32 [4096, 1024], P('tp', 'shard'), may hold values from 196.608 to 2621.44
- vectors: float32 [13, 1024], P(None, 'shard'), may hold values from -0.9 to 1.6
- m_vectors: float32 [13, 1024], P(None, 'shard'), may hold values from -146.32365 to 146.32365
- v_vectors: float32 [13, 1024], P(None, 'shard'), may hold values from 49.152 to 78643.2
Outputs:
- outputs: bfloat16 [16384, 1024], P(('shard', 'ctx'))
- input_grad: float32 [16384, 1024], P(('shard', 'ctx'))
- first_qkv: float32 [3, 1024, 1024], P(None, 'shard', 'tp')
- second_qkv: float32 [3, 1024, 1024], P(None, 'shard', 'tp')
- new_qkv: float32 [3, 1024, 1024], P(None, 'shard', 'tp')
- first_dense: float32 [1024, 1024], P('tp', 'shard')
- second_dense: float32 [1024, 1024], P('tp', 'shard')
- new_dense: float32 [1024, 1024], P('tp', 'shard')
- first_fc1: float32 [1024, 4096], P('shard', 'tp')
- second_fc1: float32 [1024, 4096], P('shard', 'tp')
- new_fc1: float32 [1024, 4096], P('shard', 'tp')
- first_fc2: float32 [4096, 1024], P('tp', 'shard')
- second_fc2: float32 [4096, 1024], P('tp', 'shard')
- new_fc2: float32 [4096, 1024], P('tp', 'shard')
- first_vectors: float32 [13, 1024], P(None, 'shard')
- second_vectors: float32 [13, 1024], P(None, 'shard')
- new_vectors: float32 [13, 1024], P(None, 'shard')
All inputs are finite; a program needn't handle non-finite values.
Results may differ from a plain program's by a relative error of at most 0.0045.
The roundings to bfloat16 on the way count: a program that leaves them out, or rounds other values in their place, can miss the bound.
Values may be sent and summed in bfloat16 or wider, within the bound.
No kernel may reach another device: no remote copies, remote signals or barrier semaphores. Data moves between devices by JAX's collectives and lax.ppermute only.
A program may use at most 192 MiB of HBM per device.

v0:
```python
import jax
import jax.numpy as jnp
from jax import lax
from jax.sharding import PartitionSpec as P

D = 1024
HD = 64
ROT = 16
FF = 4096
STEP = 10


norm_eps = 1e-05
rope_base = 10000.0
masked_score = -1e30
beta_one = 0.9
beta_two = 0.95
adam_eps = 1e-08
rate_matrix = 0.05
rate_vector = 0.5
weight_decay = 0.01


def layer_norm(value, gain, shift):
    centre = value - jnp.mean(value, axis=-1, keepdims=True)
    spread = jnp.mean(centre * centre, axis=-1, keepdims=True)
    return centre * lax.rsqrt(spread + norm_eps) * gain + shift


def rope_tables(length, rotary):
    half = rotary // 2
    frequency = rope_base ** (-(jnp.arange(half, dtype=jnp.float32) * 2.0) / rotary)
    angle = jnp.arange(length, dtype=jnp.float32)[:, None] * frequency[None, :]
    return (jnp.cos(angle), jnp.sin(angle))


def rotate(value, cosine, sine):
    half = cosine.shape[1]
    first = value[..., :half]
    second = value[..., half : 2 * half]
    cos_part = cosine[:, None, :]
    sin_part = sine[:, None, :]
    return jnp.concatenate(
        [
            first * cos_part - second * sin_part,
            second * cos_part + first * sin_part,
            value[..., 2 * half :],
        ],
        axis=-1,
    )


def masked_scores(query_block, key_rot, start, scale):
    raw = (
        jnp.einsum("qhd,khd->hqk", query_block, key_rot, preferred_element_type=jnp.float32) * scale
    )
    rows = start + jnp.arange(query_block.shape[0], dtype=jnp.int32)
    columns = jnp.arange(key_rot.shape[0], dtype=jnp.int32)
    return jnp.where(columns[None, None, :] <= rows[None, :, None], raw, masked_score)


def adam(weight, first, second, gradient, rate, decay):
    first_new = beta_one * first + (1.0 - beta_one) * gradient
    second_new = beta_two * second + (1.0 - beta_two) * gradient * gradient
    scaled = (
        first_new
        / (1.0 - beta_one**STEP)
        / (jnp.sqrt(second_new / (1.0 - beta_two**STEP)) + adam_eps)
    )
    return (first_new, second_new, weight - rate * (scaled + decay * weight))


def gelu_exact(operand):
    return jax.nn.gelu(operand, approximate=False)


def body(
    inputs,
    cotangent,
    w_qkv,
    m_qkv,
    v_qkv,
    w_dense,
    m_dense,
    v_dense,
    w_fc1,
    m_fc1,
    v_fc1,
    w_fc2,
    m_fc2,
    v_fc2,
    vectors,
    m_vectors,
    v_vectors,
):
    tp_index = lax.axis_index("tp")
    ctx_count = lax.axis_size("ctx")
    low_qkv = w_qkv.astype(jnp.bfloat16)
    low_dense = w_dense.astype(jnp.bfloat16)
    low_fc1 = w_fc1.astype(jnp.bfloat16)
    low_fc2 = w_fc2.astype(jnp.bfloat16)
    low_vectors = vectors.astype(jnp.bfloat16)
    full_qkv, full_dense, full_fc1, full_fc2, full_vectors = (
        lax.all_gather(low_qkv, "shard", axis=1, tiled=True),
        lax.all_gather(low_dense, "shard", axis=1, tiled=True),
        lax.all_gather(low_fc1, "shard", axis=0, tiled=True),
        lax.all_gather(low_fc2, "shard", axis=1, tiled=True),
        lax.all_gather(low_vectors, "shard", axis=1, tiled=True),
    )
    width = inputs.shape[1]
    tok_count = inputs.shape[0]
    head_cols = full_qkv.shape[2]
    unit_cols = full_fc1.shape[1]
    fc1_rows = FF // D
    vec_rows = full_vectors.astype(jnp.float32)
    bias_qkv = lax.dynamic_slice_in_dim(vec_rows[0:3], tp_index * head_cols, head_cols, 1)
    bias_dense = vec_rows[3]
    bias_fc1 = lax.dynamic_slice_in_dim(
        vec_rows[4 : 4 + fc1_rows].reshape(-1), tp_index * unit_cols, unit_cols, 0
    )
    bias_fc2 = vec_rows[4 + fc1_rows]
    gain_one = vec_rows[5 + fc1_rows]
    shift_one = vec_rows[6 + fc1_rows]
    gain_two = vec_rows[7 + fc1_rows]
    shift_two = vec_rows[8 + fc1_rows]
    tokens = inputs.astype(jnp.float32)
    normed_one = layer_norm(tokens, gain_one, shift_one).astype(jnp.bfloat16)
    normed_two = layer_norm(tokens, gain_two, shift_two).astype(jnp.bfloat16)
    projected = (
        jnp.einsum("td,kde->tke", normed_one, full_qkv, preferred_element_type=jnp.float32)
        + bias_qkv[None]
    ).astype(jnp.bfloat16)
    local_cols = head_cols // ctx_count
    arriving = lax.all_to_all(
        projected.reshape(tok_count, 3, ctx_count, local_cols),
        "ctx",
        split_axis=2,
        concat_axis=0,
        tiled=True,
    )
    seq_len = tok_count * ctx_count
    heads_here = local_cols // HD
    per_head = arriving.reshape(seq_len, 3, heads_here, HD)
    cosine, sine = rope_tables(seq_len, ROT)
    query_rot = rotate(per_head[:, 0].astype(jnp.float32), cosine, sine).astype(jnp.bfloat16)
    key_rot = rotate(per_head[:, 1].astype(jnp.float32), cosine, sine).astype(jnp.bfloat16)
    value = per_head[:, 2]
    block = min(512, seq_len)
    starts = jnp.arange(seq_len // block, dtype=jnp.int32) * block
    scale = HD ** (-0.5)

    def forward_block(start):
        query_block = lax.dynamic_slice_in_dim(query_rot, start, block, 0)
        scores = masked_scores(query_block, key_rot, start, scale)
        top = jnp.max(scores, axis=-1, keepdims=True)
        exponent = jnp.exp(scores - top)
        total = jnp.sum(exponent, axis=-1, keepdims=True)
        shares = (exponent / total).astype(jnp.bfloat16)
        result = jnp.einsum("hqk,khd->qhd", shares, value, preferred_element_type=jnp.float32)
        return (result.astype(jnp.bfloat16), (top + jnp.log(total))[..., 0])

    attended, log_norm = lax.map(forward_block, starts)
    returning = lax.all_to_all(
        attended.reshape(seq_len, 1, local_cols), "ctx", split_axis=0, concat_axis=1, tiled=True
    )
    attended_tok = returning.reshape(tok_count, head_cols)
    hidden = jnp.dot(normed_two, full_fc1, preferred_element_type=jnp.float32) + bias_fc1
    activated = gelu_exact(hidden).astype(jnp.bfloat16)
    partial_value = jnp.dot(attended_tok, full_dense, preferred_element_type=jnp.float32) + jnp.dot(
        activated, full_fc2, preferred_element_type=jnp.float32
    )
    summed = lax.psum(partial_value, "tp")
    outputs = (tokens + summed + bias_dense + bias_fc2).astype(jnp.bfloat16)
    full_qkv, full_dense, full_fc1, full_fc2 = (
        lax.all_gather(low_qkv, "shard", axis=1, tiled=True),
        lax.all_gather(low_dense, "shard", axis=1, tiled=True),
        lax.all_gather(low_fc1, "shard", axis=0, tiled=True),
        lax.all_gather(low_fc2, "shard", axis=1, tiled=True),
    )
    back_float = cotangent.astype(jnp.float32)
    grad_dense = jnp.einsum(
        "te,td->ed", attended_tok, cotangent, preferred_element_type=jnp.float32
    )
    grad_fc2 = jnp.einsum("tu,td->ud", activated, cotangent, preferred_element_type=jnp.float32)
    bias_back = jnp.sum(back_float, axis=0)
    d_attended = jnp.einsum(
        "td,ed->te", cotangent, full_dense, preferred_element_type=jnp.float32
    ).astype(jnp.bfloat16)
    d_activated = jnp.einsum("td,ud->tu", cotangent, full_fc2, preferred_element_type=jnp.float32)
    d_hidden = jax.vjp(gelu_exact, hidden)[1](d_activated)[0].astype(jnp.bfloat16)
    heads_grad = lax.all_to_all(
        d_attended.reshape(tok_count, ctx_count, local_cols),
        "ctx",
        split_axis=1,
        concat_axis=0,
        tiled=True,
    )
    d_heads = heads_grad.reshape(seq_len, heads_here, HD)

    def backward_block(carry, pair):
        d_key, d_value = carry
        start, log_block = pair
        query_block = lax.dynamic_slice_in_dim(query_rot, start, block, 0)
        grad_block = lax.dynamic_slice_in_dim(d_heads, start, block, 0)
        scores = masked_scores(query_block, key_rot, start, scale)
        shares = jnp.exp(scores - log_block[..., None])
        d_shares = jnp.einsum("qhd,khd->hqk", grad_block, value, preferred_element_type=jnp.float32)
        inner = jnp.sum(shares * d_shares, axis=-1, keepdims=True)
        d_scores = (shares * (d_shares - inner)).astype(jnp.bfloat16)
        d_query = (
            jnp.einsum("hqk,khd->qhd", d_scores, key_rot, preferred_element_type=jnp.float32)
            * scale
        )
        d_key = (
            d_key
            + jnp.einsum("hqk,qhd->khd", d_scores, query_block, preferred_element_type=jnp.float32)
            * scale
        )
        d_value = d_value + jnp.einsum(
            "hqk,qhd->khd",
            shares.astype(jnp.bfloat16),
            grad_block,
            preferred_element_type=jnp.float32,
        )
        return ((d_key, d_value), d_query)

    empty = jnp.zeros((seq_len, heads_here, HD), jnp.float32)
    (d_key, d_value), d_query = lax.scan(backward_block, (empty, empty), (starts, log_norm))
    unrotate = jax.vjp(lambda operand: rotate(operand, cosine, sine), empty)[1]
    d_query = unrotate(d_query.reshape(seq_len, heads_here, HD))[0]
    d_key = unrotate(d_key)[0]
    stacked = (
        jnp.stack([d_query, d_key, d_value], axis=1)
        .reshape(seq_len, 3, 1, local_cols)
        .astype(jnp.bfloat16)
    )
    leaving = lax.all_to_all(stacked, "ctx", split_axis=0, concat_axis=2, tiled=True)
    d_projected = leaving.reshape(tok_count, 3, head_cols)
    grad_qkv = jnp.einsum(
        "td,tke->kde", normed_one, d_projected, preferred_element_type=jnp.float32
    )
    d_normed_one = jnp.einsum(
        "tke,kde->td", d_projected, full_qkv, preferred_element_type=jnp.float32
    )
    grad_fc1 = jnp.einsum("td,tu->du", normed_two, d_hidden, preferred_element_type=jnp.float32)
    d_normed_two = jnp.einsum("tu,du->td", d_hidden, full_fc1, preferred_element_type=jnp.float32)
    bias_qkv_grad = jnp.sum(d_projected.astype(jnp.float32), axis=0)
    bias_fc1_grad = jnp.sum(d_hidden.astype(jnp.float32), axis=0)
    placed_qkv = lax.dynamic_update_slice_in_dim(
        jnp.zeros((3, width), jnp.float32), bias_qkv_grad, tp_index * head_cols, 1
    )
    placed_fc1 = lax.dynamic_update_slice_in_dim(
        jnp.zeros((FF,), jnp.float32), bias_fc1_grad, tp_index * unit_cols, 0
    ).reshape(fc1_rows, width)
    bias_rows = jnp.concatenate([placed_qkv, placed_fc1], axis=0)
    d_normed_one, d_normed_two, bias_rows = lax.psum((d_normed_one, d_normed_two, bias_rows), "tp")
    d_tokens_one, d_gain_one, d_shift_one = jax.vjp(layer_norm, tokens, gain_one, shift_one)[1](
        d_normed_one
    )
    d_tokens_two, d_gain_two, d_shift_two = jax.vjp(layer_norm, tokens, gain_two, shift_two)[1](
        d_normed_two
    )
    d_tokens = d_tokens_one + d_tokens_two
    norm_rows = jnp.stack([d_gain_one, d_shift_one, d_gain_two, d_shift_two], axis=0)
    input_grad = back_float + d_tokens
    grad_vectors = jnp.concatenate(
        [bias_rows[0:3], bias_back[None], bias_rows[3:], bias_back[None], norm_rows], axis=0
    )
    owned = (
        lax.psum_scatter(grad_qkv, "shard", scatter_dimension=1, tiled=True),
        lax.psum_scatter(grad_dense, "shard", scatter_dimension=1, tiled=True),
        lax.psum_scatter(grad_fc1, "shard", scatter_dimension=0, tiled=True),
        lax.psum_scatter(grad_fc2, "shard", scatter_dimension=1, tiled=True),
        lax.psum_scatter(grad_vectors, "shard", scatter_dimension=1, tiled=True),
    )
    owned = lax.psum((owned[0], owned[1], owned[2], owned[3], owned[4]), "ctx")
    results = [outputs, input_grad]
    updates = (
        (w_qkv, m_qkv, v_qkv, rate_matrix, weight_decay),
        (w_dense, m_dense, v_dense, rate_matrix, weight_decay),
        (w_fc1, m_fc1, v_fc1, rate_matrix, weight_decay),
        (w_fc2, m_fc2, v_fc2, rate_matrix, weight_decay),
        (vectors, m_vectors, v_vectors, rate_vector, 0.0),
    )
    for position, entry in enumerate(updates):
        results.extend(adam(entry[0], entry[1], entry[2], owned[position], entry[3], entry[4]))
    return tuple(results)


def solution(mesh):
    placed = (
        P(("shard", "ctx"), None),
        P(("shard", "ctx"), None),
        P(None, "shard", "tp"),
        P(None, "shard", "tp"),
        P(None, "shard", "tp"),
        P("tp", "shard"),
        P("tp", "shard"),
        P("tp", "shard"),
        P("shard", "tp"),
        P("shard", "tp"),
        P("shard", "tp"),
        P("tp", "shard"),
        P("tp", "shard"),
        P("tp", "shard"),
        P(None, "shard"),
        P(None, "shard"),
        P(None, "shard"),
    )
    return jax.shard_map(
        body,
        mesh=mesh,
        in_specs=placed,
        out_specs=(
            P(("shard", "ctx"), None),
            P(("shard", "ctx"), None),
            P(None, "shard", "tp"),
            P(None, "shard", "tp"),
            P(None, "shard", "tp"),
            P("tp", "shard"),
            P("tp", "shard"),
            P("tp", "shard"),
            P("shard", "tp"),
            P("shard", "tp"),
            P("shard", "tp"),
            P("tp", "shard"),
            P("tp", "shard"),
            P("tp", "shard"),
            P(None, "shard"),
            P(None, "shard"),
            P(None, "shard"),
        ),
        check_vma=False,
    )
```

profile of v0, /device:TPU:0, one launch (start us, length us, event | category | flops | bytes accessed | tf_op | source)
XLA Modules:
  0.0 1418.1 jit_solution(11039029974120088277)
XLA Ops:
  13.6 28.0 %all_gather.19 = bf16[13,1024]{1,0:T(8,128)(2,1)S(1)} all-gather(bf16[13,128]{1,0:T(8,128)(2,1)S(1)} %convert_element_type.91), channel_id=1, replica_groups=mesh['shard'=8,'ctx'=2,'tp'=2] {'shard'}, dimensions={1}, use_global_device_ids=true | all-gather | bytes 29952 | tf_op jit(solution)/shard_map/all_gather | solution.py:108
  43.8 9.2 all-gather.7.cloned.1.call-done
  60.8 56.9 %all-gather.5.cloned.1.call-done = bf16[3,1024,512]{1,2,0:T(8,128)(2,1)} async-done(((bf16[3,128,512]{1,2,0:T(8,128)(2,1)}), bf16[3,1024,512]{1,2,0:T(8,128)(2,1)}) %all-gather.5.cloned.1.call-update) | async-done | bytes 3145744 | tf_op jit(solution)/shard_map/all_gather | solution.py:104
  117.7 5.6 add_convert_fusion.1
  139.5 26.7 %all-to-all-done = bf16[1024,3,2,256]{0,3,1,2:T(8,128)(2,1)S(1)} async-done(((bf16[1024,3,2,256]{0,3,1,2:T(8,128)(2,1)}), bf16[1024,3,2,256]{0,3,1,2:T(8,128)(2,1)S(1)}, u32[]{:S(2)}, u32[]{:S(2)}) %all-to-all-start) | async-done | bytes 3145760 | tf_op jit(solution)/shard_map/all_to_all | solution.py:134
  166.2 4.9 copy.106
  171.1 6.1 reshape.310
  181.4 75.2 %while.27 = (s32[]{:T(128)}, bf16[4,512,4,64]{1,3,2,0:T(8,128)(2,1)}, f32[4,4,512]{2,1,0:T(4,128)S(1)}, s32[4]{0:T(128)S(1)}, bf16[2048,4,64]{0,2,1:T(8,128)(2,1...) while((s32[]{:T(128)}, ...), condition=%wide.region_5.6_spmd, body=%wide.region_2.5_spmd.sunk | while | flops 1125251584 | bytes 57217692 | solution.py:162
  185.2 4.6 fusion.143
  194.2 5.9 fusion.145
  213.0 5.9 fusion.145
  231.8 5.9 fusion.145
  250.6 5.9 fusion.145
  256.5 288.1 %while.28 = (s32[]{:T(128)}, f32[2048,4,64]{0,2,1:T(8,128)}, f32[2048,4,64]{0,2,1:T(8,128)}, f32[4,512,4,64]{1,0,3,2:T(4,128)}, s32[4]{0:T(128)S(1)}, /*index=5*...) while((s32[]{:T(128)}, f32[2048,4,64]{0,2,1:T(8,128)}, ...), condition=%wide.region_9.10_spmd.clone, body=%wide.region_7.9_spmd.clone.sunk | while | flops 2751068672 | bytes 187232528 | solution.py:228
  259.6 9.2 fusion.155
  270.1 12.5 multiply_reduce_fusion.2
  282.6 12.1 multiply_convert_fusion.3
  298.5 11.1 dynamic_update_slice.29
  309.6 6.5 fusion.156
  316.1 11.9 fusion.157
  330.6 9.2 fusion.155
  341.1 12.5 multiply_reduce_fusion.2
  353.6 12.1 multiply_convert_fusion.3
  369.5 11.1 dynamic_update_slice.29
  380.6 7.1 fusion.156
  387.7 12.5 fusion.157
  402.8 9.2 fusion.155
  413.3 12.5 multiply_reduce_fusion.2
  425.8 12.1 multiply_convert_fusion.3
  441.7 11.1 dynamic_update_slice.29
  452.8 7.1 fusion.156
  459.9 12.5 fusion.157
  475.0 9.2 fusion.155
  485.5 12.5 multiply_reduce_fusion.2
  498.0 12.1 multiply_convert_fusion.3
  513.9 11.1 dynamic_update_slice.29
  525.0 7.0 fusion.156
  532.0 12.5 fusion.157
  551.8 4.8 copy.112
  563.7 11.8 reduce.2
  580.3 9.4 fusion.79
  589.6 28.0 %convert_reduce_fusion = (f32[2048]{0:T(1024)S(1)}, bf16[1024,2048]{1,0:T(8,128)(2,1)}, f32[1024,2048]{1,0:T(8,128)}) fusion(f32[1024,2048]{1,0:T(8,128)} %fusion.79, f32[2048]{0:T(1024)S(1)} %copy-done.40, bf16[1024,1024]{1,0:T(8,128)(2,1)} %param.22, bf16[2048,1024]{1,0:T(8,128)(2,1)} %all-gather.11.cloned.1.call-done), kind=kOutput, calls=%fused_computation.47 | convolution fusion | flops 4452251648 | bytes 27279360 | tf_op jit(solution)/shard_map/td,ud->tu/dot_general | solution.py:189
  617.6 10.1 multiply_convert_fusion.1
  627.7 5.6 all-to-all-start.3
  633.4 10.0 fusion.92
  643.4 6.5 fusion.93
  656.0 5.8 convolution_add_fusion
  661.8 17.9 %all-to-all-done.3 = bf16[2048,3,1,256]{3,1,2,0:T(4,128)(2,1)} async-done(((bf16[2048,3,1,256]{3,1,2,0:T(4,128)(2,1)}), bf16[2048,3,1,256]{3,1,2,0:T(4,128)(2,1)}, u32[]{:S(2)}, u32[]{:S(2)}) %all-to-all-start.3) | async-done | bytes 3145760 | tf_op jit(solution)/shard_map/all_to_all | solution.py:237
  684.0 4.9 copy.114
  688.9 6.0 reshape.317
  694.9 8.3 convolution_bitcast_fusion.1
  707.6 8.1 convolution_bitcast_fusion
  715.8 12.3 fusion.95
  728.1 9.7 fusion.77
  744.3 7.3 all-reduce.11.cloned.1.call-done
  751.7 5.2 fusion.84
  761.6 5.3 convert_reduce_fusion.3
  768.3 56.2 %reduce-scatter.8.cloned.1.call-done = f32[512,128]{1,0:T(8,128)} async-done(((f32[512,1024]{1,0:T(8,128)}), f32[512,128]{1,0:T(8,128)}) %reduce-scatter.8.cloned.1.call-update) | async-done | bytes 262160 | tf_op jit(solution)/shard_map/reduce_scatter | solution.py:271
  824.6 121.0 %reduce-scatter.6.cloned.1.call-done = f32[3,128,512]{1,2,0:T(8,128)} async-done(((f32[3,1024,512]{1,2,0:T(8,128)}), f32[3,128,512]{1,2,0:T(8,128)}) %reduce-scatter.6.cloned.1.call-update) | async-done | bytes 786448 | tf_op jit(solution)/shard_map/reduce_scatter | solution.py:270
  945.5 152.2 %reduce-scatter.12.cloned.1.call-done = f32[2048,128]{1,0:T(8,128)} async-done(((f32[2048,1024]{1,0:T(8,128)}), f32[2048,128]{1,0:T(8,128)}) %reduce-scatter.12.cloned.1.call-update) | async-done | bytes 1048592 | tf_op jit(solution)/shard_map/reduce_scatter | solution.py:273
  1097.8 152.1 %reduce-scatter.10.cloned.1.call-done = f32[128,2048]{1,0:T(8,128)} async-done(((f32[1024,2048]{1,0:T(8,128)}), f32[128,2048]{1,0:T(8,128)}) %reduce-scatter.10.cloned.1.call-update) | async-done | bytes 1048592 | tf_op jit(solution)/shard_map/reduce_scatter | solution.py:272
  1250.5 55.7 %reduce-scatter.14.cloned.1.call-done = f32[13,128]{1,0:T(8,128)} async-done(((f32[13,1024]{1,0:T(8,128)}), f32[13,128]{1,0:T(8,128)}) %reduce-scatter.14.cloned.1.call-update) | async-done | bytes 6672 | tf_op jit(solution)/shard_map/reduce_scatter | solution.py:274
  1306.1 5.1 psum.71
  1311.9 82.1 %all-reduce.13.cloned.1.call-done = (f32[3,128,512]{1,2,0:T(8,128)}, f32[512,128]{1,0:T(8,128)}, f32[128,2048]{1,0:T(8,128)}, f32[2048,128]{1,0:T(8,128)}) async-done(((f32[3,128,512]{1,2,0:T(8,128)}, f32[512,128]{1,0:T(8,128)}, f32[128,2048]{1,0:T(8,128)}, f32[2048,128]{1,0:T(8,128)}), (f32[3,128,512]{1,2,0:T(8,128)}, f32[512,128]{1,0:T(8,128)}, f32[128,2048]{1,0:T(8,128)}, ...) | async-done | bytes 3145744 | tf_op jit(solution)/shard_map/psum | solution.py:276
  (277 shorter events, 163.2 us)
Async XLA Ops:
  7.2 6.4 copy-start.41
  7.2 34.4 %copy-start.2 = (bf16[1024,1024]{1,0:T(8,128)(2,1)S(1)}, bf16[1024,1024]{1,0:T(8,128)(2,1)}, u32[]{:S(2)}) copy-start(bf16[1024,1024]{1,0:T(8,128)(2,1)} %param.21) | copy-start | bytes 6291460
  7.2 45.9 %all-gather.7.cloned.1.call-start = ((), (), s32[]{:S(2)}) async-start(), calls=%async_computation.10 | async-start | bytes 1179648 | tf_op jit(solution)/shard_map/all_gather | solution.py:105
  9.0 108.7 %all-gather.5.cloned.1.call-start = ((), (), s32[]{:S(2)}) async-start(), calls=%async_computation.9 | async-start | bytes 3538944 | tf_op jit(solution)/shard_map/all_gather | solution.py:104
  10.5 46.7 %copy-start.10 = (f32[3,128,512]{1,2,0:T(8,128)}, f32[3,128,512]{1,2,0:T(8,128)S(1)}, u32[]{:S(2)}) copy-start(f32[3,128,512]{1,2,0:T(8,128)S(1)} %copy.104) | copy-start | bytes 2359300
  11.4 568.8 %all-gather.9.cloned.1.call-start = ((), (), s32[]{:S(2)}) async-start(), calls=%async_computation.11 | async-start | bytes 4718592 | tf_op jit(solution)/shard_map/all_gather | solution.py:106
  41.9 75.8 %copy-start.31 = (f32[1024]{0:T(1024)}, f32[1024]{0:T(1024)S(1)}, u32[]{:S(2)}) copy-start(f32[1024]{0:T(1024)S(1)} %broadcast_multiply_fusion) | copy-start | bytes 12292
  43.2 74.5 %copy-start.36 = (f32[1024]{0:T(1024)}, f32[1024]{0:T(1024)S(1)}, u32[]{:S(2)}) copy-start(f32[1024]{0:T(1024)S(1)} %fusion.74) | copy-start | bytes 12292
  43.8 73.9 %copy-start.33 = (f32[1,1024]{1,0:T(1,128)}, f32[1,1024]{1,0:T(1,128)S(1)}, u32[]{:S(2)}) copy-start(f32[1,1024]{1,0:T(1,128)S(1)} %get-tuple-element.329) | copy-start | bytes 12292
  43.8 73.9 %copy-start.48 = (f32[1,1024]{1,0:T(1,128)}, f32[1,1024]{1,0:T(1,128)S(1)}, u32[]{:S(2)}) copy-start(f32[1,1024]{1,0:T(1,128)S(1)} %get-tuple-element.330) | copy-start | bytes 12292
  57.2 68.1 %all-to-all-start.2 = ((bf16[1024,2,256]{0,2,1:T(8,128)(2,1)}), bf16[1024,2,256]{0,2,1:T(8,128)(2,1)S(1)}, u32[]{:S(2)}, u32[]{:S(2)}) async-start(bf16[1024,2,256]{0,2,1:T(8,128)(2,1)} %bitcast.154), calls=%async_computation.2 | async-start | bytes 2097152 | tf_op jit(solution)/shard_map/all_to_all | solution.py:191
  126.3 40.0 %all-to-all-start = ((bf16[1024,3,2,256]{0,3,1,2:T(8,128)(2,1)}), bf16[1024,3,2,256]{0,3,1,2:T(8,128)(2,1)S(1)}, u32[]{:S(2)}, u32[]{:S(2)}) async-start(bf16[1024,3,2,256]{0,3,1,2:T(8,128)(2,1)} %copy.105), calls=%async_computation | async-start | bytes 6291456 | tf_op jit(solution)/shard_map/all_to_all | solution.py:134
  130.2 459.4 %all-gather.11.cloned.1.call-start = ((), (), s32[]{:S(2)}) async-start(), calls=%async_computation.12 | async-start | bytes 4718592 | tf_op jit(solution)/shard_map/all_gather | solution.py:107
  133.6 46.5 %copy-start.23 = (f32[2048,8]{0,1:T(8,128)}, f32[2048,8]{0,1:T(8,128)S(1)}, u32[]{:S(2)}) copy-start(f32[2048,8]{0,1:T(8,128)S(1)} %get-tuple-element.335) | copy-start | bytes 196612
  133.6 46.5 %copy-start.25 = (f32[2048,8]{0,1:T(8,128)}, f32[2048,8]{0,1:T(8,128)S(1)}, u32[]{:S(2)}) copy-start(f32[2048,8]{0,1:T(8,128)S(1)} %get-tuple-element.336) | copy-start | bytes 196612
  256.9 13.2 copy-start.4
  294.7 3.3 copy-start
  316.1 11.9 copy-start.5
  328.0 13.1 copy-start.4
  387.7 12.5 copy-start.5
  400.2 13.1 copy-start.4
  459.9 12.5 copy-start.5
  472.4 13.1 copy-start.4
  532.0 12.5 copy-start.5
  544.6 3.8 copy-start.1
  563.1 17.1 %copy-start.3 = (bf16[1024,1024]{1,0:T(8,128)(2,1)S(1)}, bf16[1024,1024]{1,0:T(8,128)(2,1)}, u32[]{:S(2)}) copy-start(bf16[1024,1024]{1,0:T(8,128)(2,1)} %param.21) | copy-start | bytes 6291460
  563.1 17.1 %copy-start.32 = (f32[1024]{0:T(1024)S(1)}, f32[1024]{0:T(1024)}, u32[]{:S(2)}) copy-start(f32[1024]{0:T(1024)} %copy-done.31) | copy-start | bytes 12292
  563.1 17.1 %copy-start.35 = (f32[1,1024]{1,0:T(1,128)S(1)}, f32[1,1024]{1,0:T(1,128)}, u32[]{:S(2)}) copy-start(f32[1,1024]{1,0:T(1,128)} %get-tuple-element.331) | copy-start | bytes 12292
  563.1 17.1 %copy-start.37 = (f32[1024]{0:T(1024)S(1)}, f32[1024]{0:T(1024)}, u32[]{:S(2)}) copy-start(f32[1024]{0:T(1024)} %copy-done.36) | copy-start | bytes 12292
  563.1 17.1 %copy-start.47 = (f32[1,1024]{1,0:T(1,128)S(1)}, f32[1,1024]{1,0:T(1,128)}, u32[]{:S(2)}) copy-start(f32[1,1024]{1,0:T(1,128)} %get-tuple-element.332) | copy-start | bytes 12292
  576.6 51.1 %all-to-all-start.1 = ((bf16[2,2,131072]{2,1,0:T(2,128)(2,1)}), bf16[2,2,131072]{2,1,0:T(2,128)(2,1)S(1)}, u32[]{:S(2)}, u32[]{:S(2)}) async-start(bf16[2,2,131072]{2,1,0:T(2,128)(2,1)} %reshape.326), calls=%async_computation.1 | async-start | bytes 2097152 | tf_op jit(solution)/shard_map/all_to_all | solution.py:163
  580.2 9.4 copy-start.40
  627.7 52.0 %all-to-all-start.3 = ((bf16[2048,3,1,256]{3,1,2,0:T(4,128)(2,1)}), bf16[2048,3,1,256]{3,1,2,0:T(4,128)(2,1)}, u32[]{:S(2)}, u32[]{:S(2)}) async-start(bf16[2048,3,1,256]{3,1,2,0:T(4,128)(2,1)} %copy.112), calls=%async_computation.3 | async-start | bytes 8388608 | tf_op jit(solution)/shard_map/all_to_all | solution.py:237
  633.3 118.3 %all-reduce.11.cloned.1.call-start = ((), (), s32[]{:S(2)}) async-start(), calls=%async_computation.18 | async-start | bytes 25165824 | tf_op jit(solution)/shard_map/psum | solution.py:172
  633.4 10.1 copy-start.50
  633.4 10.1 copy-start.51
  703.3 4.3 copy-start.34
  703.3 4.3 copy-start.49
  703.3 121.3 %reduce-scatter.8.cloned.1.call-start = ((), (), s32[]{:S(2)}) async-start(), calls=%async_computation.14 | async-start | bytes 2359296 | tf_op jit(solution)/shard_map/reduce_scatter | solution.py:271
  707.6 238.0 %reduce-scatter.6.cloned.1.call-start = ((), (), s32[]{:S(2)}) async-start(), calls=%async_computation.13 | async-start | bytes 7077888 | tf_op jit(solution)/shard_map/reduce_scatter | solution.py:270
  715.7 382.1 %reduce-scatter.12.cloned.1.call-start = ((), (), s32[]{:S(2)}) async-start(), calls=%async_computation.16 | async-start | bytes 9437184 | tf_op jit(solution)/shard_map/reduce_scatter | solution.py:273
  728.0 521.8 %reduce-scatter.10.cloned.1.call-start = ((), (), s32[]{:S(2)}) async-start(), calls=%async_computation.15 | async-start | bytes 9437184 | tf_op jit(solution)/shard_map/reduce_scatter | solution.py:272
  737.8 568.3 %reduce-scatter.14.cloned.1.call-start = ((), (), s32[]{:S(2)}) async-start(), calls=%async_computation.17 | async-start | bytes 73728 | tf_op jit(solution)/shard_map/reduce_scatter | solution.py:274
  744.3 12.6 copy-start.30
  751.7 5.2 copy-start.39
  751.7 5.3 copy-start.6
  751.7 5.9 copy-start.7
  757.6 4.0 copy-start.15
  757.6 4.0 copy-start.16
  757.6 4.0 copy-start.43
  757.6 4.0 copy-start.44
  761.6 5.4 slice-start.1
  761.6 488.3 %copy-start.21 = (f32[3,128,512]{2,1,0:T(8,128)S(1)}, f32[3,128,512]{2,1,0:T(8,128)}, u32[]{:S(2)}) copy-start(f32[3,128,512]{2,1,0:T(8,128)} %param.24) | copy-start | bytes 2359300
  766.9 483.2 %copy-start.22 = (f32[3,128,512]{2,1,0:T(8,128)S(1)}, f32[3,128,512]{2,1,0:T(8,128)}, u32[]{:S(2)}) copy-start(f32[3,128,512]{2,1,0:T(8,128)} %param.25) | copy-start | bytes 2359300
  766.9 544.3 %copy-start.42 = (f32[13,128]{1,0:T(8,128)S(1)}, f32[13,128]{1,0:T(8,128)}, u32[]{:S(2)}) copy-start(f32[13,128]{1,0:T(8,128)} %param.35) | copy-start | bytes 19972
  767.0 544.3 %copy-start.45 = (f32[13,128]{1,0:T(8,128)S(1)}, f32[13,128]{1,0:T(8,128)}, u32[]{:S(2)}) copy-start(f32[13,128]{1,0:T(8,128)} %param.37) | copy-start | bytes 19972
  767.0 544.3 %copy-start.46 = (f32[13,128]{1,0:T(8,128)S(1)}, f32[13,128]{1,0:T(8,128)}, u32[]{:S(2)}) copy-start(f32[13,128]{1,0:T(8,128)} %param.36) | copy-start | bytes 19972
  767.0 627.0 %copy-start.11 = (f32[3,128,512]{1,2,0:T(8,128)S(1)}, f32[3,128,512]{1,2,0:T(8,128)}, u32[]{:S(2)}) copy-start(f32[3,128,512]{1,2,0:T(8,128)} %copy-done.10) | copy-start | bytes 2359300
  768.3 625.7 %all-reduce.13.cloned.1.call-start = ((), (), s32[]{:S(2)}) async-start(), calls=%async_computation.19 | async-start | bytes 6291456 | tf_op jit(solution)/shard_map/psum | solution.py:276
  1394.0 9.9 copy-start.12
  1401.5 6.6 copy-start.13
  1403.9 4.2 copy-start.17
  1403.9 4.2 copy-start.18
  1403.9 4.2 copy-start.19
  (14 other events, 31.6 us)
Sparse Core Ops, SparseCore 0:
  10.7 42.3 all-gather.6
  55.7 61.9 all-gather.4
  120.4 71.5 all-gather.8
  194.5 73.3 all-gather.10
  703.4 48.2 all-reduce.10
  755.0 69.4 reduce-scatter.7
  828.2 117.3 reduce-scatter.5
  949.2 148.5 reduce-scatter.11
  1101.9 147.9 reduce-scatter.9
  1253.4 52.6 reduce-scatter.13
  1308.6 85.3 all-reduce.12
where the time goes:
time: 1430 us; the launch traced here: 1420 us
  waiting for transfers between devices  738 us (52%)
  matrix products  329 us (23%)
  other arithmetic  141 us (10%)
  local copies, waits for them, and re-layouts  126 us (9%)
  blocking collectives  36.5 us (3%)
  starting transfers between devices  17.4 us (1%)
  loops' own time  16.5 us (1%)
  between operations  14.9 us (1%)
    reduce_scatter x1, waiting for transfers between devices, body(): lax.psum_scatter(grad_fc2, 'shard', scatter_dimension=1, tiled=True)  152 us
    reduce_scatter x1, waiting for transfers between devices, body(): lax.psum_scatter(grad_fc1, 'shard', scatter_dimension=0, tiled=True)  152 us
    reduce_scatter x1, waiting for transfers between devices, body(): lax.psum_scatter(grad_qkv, 'shard', scatter_dimension=1, tiled=True)  121 us
    psum x1, waiting for transfers between devices, body(): owned = lax.psum((owned[0], owned[1], owned[2], owned[3], owned[4]), 'ctx')  82.1 us
    all_gather x1, waiting for transfers between devices, body(): lax.all_gather(low_qkv, 'shard', axis=1, tiled=True)  56.9 us
    reduce_scatter x1, waiting for transfers between devices, body(): lax.psum_scatter(grad_dense, 'shard', scatter_dimension=1, tiled=True)  56.2 us
    reduce_scatter x1, waiting for transfers between devices, body(): lax.psum_scatter(grad_vectors, 'shard', scatter_dimension=1, tiled=True)  55.7 us
    dot_general x8, matrix products, masked_scores(): jnp.einsum('qhd,khd->hqk', query_block, key_rot, preferred_element_type=j...  55.3 us
  transfers between devices with their start and end apart: 15, of which 11 were waited for; matrix products, arithmetic and copies ran while one was open for 39% of the time, Pallas kernels for 0%

commit v1 on v0

v1 whole, which is shorter than its diff:
```python
import functools

import jax
import jax.numpy as jnp
from jax import lax
from jax.experimental import pallas as pl
from jax.experimental.pallas import tpu as pltpu
from jax.sharding import PartitionSpec as P

D = 1024
HD = 64
ROT = 16
FF = 4096
STEP = 10

norm_eps = 1e-05
rope_base = 10000.0
masked_score = -1e30
beta_one = 0.9
beta_two = 0.95
adam_eps = 1e-08
rate_matrix = 0.05
rate_vector = 0.5
weight_decay = 0.01

BQ = 512
BK = 512
UNIT_BLOCK = 256
VMEM = 56 * 1024 * 1024

bf16 = jnp.bfloat16
f32 = jnp.float32


def dot(a, b, contract):
    return lax.dot_general(a, b, (contract, ((), ())), preferred_element_type=f32)


NN = ((1,), (0,))
NT = ((1,), (1,))
TN = ((0,), (0,))


def swap(value, axis, mask):
    return lax.ppermute(value, axis, [(i, i ^ mask) for i in range(lax.axis_size(axis))])


def pick(value, index, axis):
    return lax.dynamic_index_in_dim(value, index, axis, keepdims=False)


def assemble(own, got, index, widths):
    _, rows, cols = own.shape

    def kernel(index_ref, own_ref, got_ref, *outs):
        for which, ref in enumerate((own_ref, got_ref)):
            for r in range(4):
                slot = index_ref[0] ^ ((r << 1) | which)
                start = 0
                for out, width in zip(outs, widths):
                    out[slot] = ref[r, :, start : start + width]
                    start += width

    vmem = pl.BlockSpec(memory_space=pltpu.VMEM)
    return pl.pallas_call(
        kernel,
        in_specs=[pl.BlockSpec(memory_space=pltpu.SMEM), vmem, vmem],
        out_specs=[vmem] * len(widths),
        out_shape=[jax.ShapeDtypeStruct((8, rows, width), bf16) for width in widths],
        compiler_params=pltpu.CompilerParams(vmem_limit_bytes=VMEM),
    )(index, own, got)


def turn(value, cosine, sine_up, sine_down, sign):
    up = pltpu.roll(value, value.shape[1] - ROT // 2, 1)
    down = pltpu.roll(value, ROT // 2, 1)
    return value * cosine + sign * (up * sine_up + down * sine_down)


def attend_kernel(
    ctx_ref, heads_ref, back_ref, cos_ref, up_ref, down_ref, heads_out, back_out,
    q_s, k_s, v_s, g_s, kt_s, vt_s, e_s, dp_s, dk_s, dv_s, dq_s, o_s, ot_s, dqt_s,
):
    step = pl.program_id(0)
    half = back_ref.shape[0] // 2
    lanes = back_ref.shape[1]
    ctx = ctx_ref[0]
    scale = HD ** (-0.5)

    @pl.when(step == 0)
    def _():
        dk_s[...] = jnp.zeros_like(dk_s)
        dv_s[...] = jnp.zeros_like(dv_s)
        for first, which in ((0, ctx), (half, 1 - ctx)):
            for at in range(0, half, BK):
                block = which * (half // BK) + at // BK
                rows = pl.ds(pl.multiple_of(block * BK, BK), BK)
                tables = (cos_ref[rows], up_ref[rows], down_ref[rows])
                here = slice(first + at, first + at + BK)
                query = turn(heads_ref[here, :lanes].astype(f32), *tables, 1.0).astype(bf16)
                q_s[rows] = (query.astype(f32) * scale).astype(bf16)
                key = turn(heads_ref[here, lanes : 2 * lanes].astype(f32), *tables, 1.0).astype(bf16)
                k_s[rows] = key
                kt_s[block] = key.astype(f32).T.astype(bf16)
                value = heads_ref[here, 2 * lanes :]
                v_s[rows] = value
                vt_s[block] = value.astype(f32).T.astype(bf16)
                g_s[rows] = back_ref[here]

    rows = pl.ds(pl.multiple_of(step * BQ, BQ), BQ)
    low_lanes = lax.broadcasted_iota(jnp.int32, (BQ, lanes), 1) < HD

    def both(value):
        value = value.astype(f32)
        return jnp.concatenate(
            [jnp.where(low_lanes, value, 0.0), jnp.where(low_lanes, 0.0, value)], axis=0
        ).astype(bf16)

    q_both = both(q_s[rows])
    g_both = both(g_s[rows])

    def keys_at(block):
        return pl.ds(pl.multiple_of(block * BK, BK), BK)

    def score(block):
        return dot(k_s[keys_at(block)], q_both, NT)

    key_row = lax.broadcasted_iota(jnp.int32, (BK, BQ), 0)
    query_col = lax.broadcasted_iota(jnp.int32, (BK, BQ), 1)
    keep = key_row <= query_col
    diagonal = score(step)
    diagonal = jnp.where(jnp.concatenate([keep, keep], axis=1), diagonal, masked_score)
    e_s[step] = diagonal
    top = jnp.max(diagonal, axis=0, keepdims=True)

    def first_pass(block, top):
        value = score(block)
        e_s[block] = value
        return jnp.maximum(top, jnp.max(value, axis=0, keepdims=True))

    top = lax.fori_loop(0, step, first_pass, top)

    def second_pass(block, carry):
        total, inner = carry
        exponent = jnp.exp(e_s[block] - top)
        d_shares = dot(v_s[keys_at(block)], g_both, NT)
        e_s[block] = exponent
        dp_s[block] = d_shares
        total = total + jnp.sum(exponent, axis=0, keepdims=True)
        inner = inner + jnp.sum(exponent * d_shares, axis=0, keepdims=True)
        return total, inner

    zero = jnp.zeros((1, 2 * BQ), f32)
    total, inner = lax.fori_loop(0, step + 1, second_pass, (zero, zero))
    inverse = 1.0 / total
    inner = inner * inverse
    ot_s[...] = jnp.zeros_like(ot_s)
    dqt_s[...] = jnp.zeros_like(dqt_s)

    def third_pass(block, carry):
        shares = e_s[block] * inverse
        low = shares.astype(bf16)
        d_scores = (shares * (dp_s[block] - inner)).astype(bf16)
        at = keys_at(block)
        dv_s[at] += dot(low, g_both, NN)
        dk_s[at] += dot(d_scores, q_both, NN)
        ot_s[...] += dot(vt_s[block], low, NN)
        dqt_s[...] += dot(kt_s[block], d_scores, NN)
        return carry

    lax.fori_loop(0, step + 1, third_pass, 0)

    def joined(ref):
        return jnp.concatenate([ref[:HD, :BQ], ref[HD:, BQ:]], axis=0).T

    o_s[rows] = joined(ot_s).astype(bf16)
    d_query = joined(dqt_s) * scale
    dq_s[rows] = turn(d_query, cos_ref[rows], up_ref[rows], down_ref[rows], -1.0).astype(bf16)

    @pl.when(step == pl.num_programs(0) - 1)
    def _():
        for first, which in ((0, ctx), (half, 1 - ctx)):
            for at in range(0, half, BK):
                here = slice(first + at, first + at + BK)
                rows = pl.ds(pl.multiple_of(which * half + at, BK), BK)
                tables = (cos_ref[rows], up_ref[rows], down_ref[rows])
                heads_out[here, :lanes] = dq_s[rows]
                heads_out[here, lanes : 2 * lanes] = turn(dk_s[rows], *tables, -1.0).astype(bf16)
                heads_out[here, 2 * lanes :] = dv_s[rows].astype(bf16)
                back_out[here] = o_s[rows]


def attend(ctx, heads, back, tables, pair):
    length = heads.shape[0]
    lanes = 2 * HD
    blocks = length // BK
    table = pl.BlockSpec((length, lanes), lambda i: (0, 0))
    return pl.pallas_call(
        attend_kernel,
        grid=(length // BQ,),
        in_specs=[
            pl.BlockSpec(memory_space=pltpu.SMEM),
            pl.BlockSpec((length, 3 * lanes), lambda i: (0, pair)),
            pl.BlockSpec((length, lanes), lambda i: (0, pair)),
            table,
            table,
            table,
        ],
        out_specs=[pl.BlockSpec((length, 3 * lanes), lambda i: (0, 0)), table],
        out_shape=[
            jax.ShapeDtypeStruct((length, 3 * lanes), bf16),
            jax.ShapeDtypeStruct((length, lanes), bf16),
        ],
        scratch_shapes=[pltpu.VMEM((length, lanes), bf16)] * 4
        + [pltpu.VMEM((blocks, lanes, BK), bf16)] * 2
        + [pltpu.VMEM((blocks, BK, 2 * BQ), f32)] * 2
        + [pltpu.VMEM((length, lanes), f32)] * 2
        + [pltpu.VMEM((length, lanes), bf16)] * 2
        + [pltpu.VMEM((lanes, 2 * BQ), f32)] * 2,
        compiler_params=pltpu.CompilerParams(vmem_limit_bytes=VMEM),
    )(ctx, heads, back, *tables)


def mlp_kernel(normed_ref, back_ref, up_ref, down_ref, bias_ref, act_ref, dh_ref, sum_ref):
    rows = normed_ref.shape[0]
    step = min(256, rows)
    total = jnp.zeros((1, up_ref.shape[1]), f32)
    for at in range(0, rows, step):
        here = slice(at, at + step)
        hidden = dot(normed_ref[here], up_ref[...], NN) + bias_ref[...]
        d_act = dot(back_ref[here], down_ref[...], NN)
        share = 0.5 * (1.0 + lax.erf(hidden * (0.5**0.5)))
        density = jnp.exp(-0.5 * hidden * hidden) * 0.3989422804014327
        act_ref[here] = (hidden * share).astype(bf16)
        d_hidden = (d_act * (share + hidden * density)).astype(bf16)
        dh_ref[here] = d_hidden
        total = total + jnp.sum(d_hidden.astype(f32), axis=0, keepdims=True)
    sum_ref[...] = total


def mlp(normed, back, up, down, bias):
    rows, width = normed.shape
    units = up.shape[1]
    whole = pl.BlockSpec((rows, width), lambda j: (0, 0))
    columns = pl.BlockSpec((width, UNIT_BLOCK), lambda j: (0, j))
    out = pl.BlockSpec((rows, UNIT_BLOCK), lambda j: (0, j))
    line = pl.BlockSpec((1, UNIT_BLOCK), lambda j: (0, j))
    return pl.pallas_call(
        mlp_kernel,
        grid=(units // UNIT_BLOCK,),
        in_specs=[whole, whole, columns, columns, line],
        out_specs=[out, out, line],
        out_shape=[
            jax.ShapeDtypeStruct((rows, units), bf16),
            jax.ShapeDtypeStruct((rows, units), bf16),
            jax.ShapeDtypeStruct((1, units), f32),
        ],
        compiler_params=pltpu.CompilerParams(vmem_limit_bytes=VMEM),
    )(normed, back, up, down, bias)


def grads_kernel(column_ref, first_ref, one_ref, second_ref, two_ref, kept_ref, sent_ref):
    value = jnp.concatenate(
        [dot(first_ref[...], one_ref[...], TN), dot(second_ref[...], two_ref[...], TN)], axis=1
    )
    rows = value.shape[0] // 2
    top, bottom = value[:rows], value[rows:]
    here = column_ref[0] == 0
    kept_ref[0] = jnp.where(here, top, bottom)
    sent_ref[0] = jnp.where(here, bottom, top).astype(bf16)


def grads(column, first, one, second, two):
    length, width = first.shape
    rows = width // 8
    cols = one.shape[1] + two.shape[1]
    left = pl.BlockSpec((length, 2 * rows), lambda i: (0, i))
    out = pl.BlockSpec((1, rows, cols), lambda i: (i, 0, 0))
    return pl.pallas_call(
        grads_kernel,
        grid=(4,),
        in_specs=[
            pl.BlockSpec(memory_space=pltpu.SMEM),
            left,
            pl.BlockSpec(one.shape, lambda i: (0, 0)),
            left,
            pl.BlockSpec(two.shape, lambda i: (0, 0)),
        ],
        out_specs=[out, out],
        out_shape=[
            jax.ShapeDtypeStruct((4, rows, cols), f32),
            jax.ShapeDtypeStruct((4, rows, cols), bf16),
        ],
        compiler_params=pltpu.CompilerParams(vmem_limit_bytes=VMEM),
    )(column, first, one, second, two)


def combine(line, kept, crossed):
    def kernel(line_ref, kept_ref, crossed_ref, own_ref, *outs):
        for r, out in zip((0, 2, 3, 1), (own_ref,) + outs):
            at = line_ref[0] ^ r
            out[...] = (kept_ref[at] + crossed_ref[at].astype(f32)).astype(out.dtype)

    vmem = pl.BlockSpec(memory_space=pltpu.VMEM)
    shape = kept.shape[1:]
    return pl.pallas_call(
        kernel,
        in_specs=[pl.BlockSpec(memory_space=pltpu.SMEM), vmem, vmem],
        out_specs=[vmem] * 4,
        out_shape=[jax.ShapeDtypeStruct(shape, f32)] + [jax.ShapeDtypeStruct(shape, bf16)] * 3,
        compiler_params=pltpu.CompilerParams(vmem_limit_bytes=VMEM),
    )(line, kept, crossed)


def finish_kernel(
    tp_ref, dh_a, dh_b, o_a, o_b, act_a, act_b, du_a, du_b, tok_ref,
    wh, wd, f1_a, f1_b, f2_a, f2_b, gain_ref, send_ref, keep_ref, norm_ref, line_ref,
):
    cut = dh_a.shape[1]
    lanes = o_a.shape[1]

    @pl.when(pl.program_id(0) == 0)
    def _():
        norm_ref[...] = jnp.zeros_like(norm_ref)
        line_ref[...] = jnp.zeros_like(line_ref)

    out = (
        dot(act_a[...], f2_a[...], NT)
        + dot(act_b[...], f2_b[...], NT)
        + dot(o_a[...], wd[:, :lanes], NT)
        + dot(o_b[...], wd[:, lanes:], NT)
    )
    one = dot(dh_a[...], wh[:, :cut], NT) + dot(dh_b[...], wh[:, cut:], NT)
    two = dot(du_a[...], f1_a[...], NT) + dot(du_b[...], f1_b[...], NT)
    tokens = tok_ref[...].astype(f32)
    centre = tokens - jnp.mean(tokens, axis=-1, keepdims=True)
    unit = centre * lax.rsqrt(jnp.mean(centre * centre, axis=-1, keepdims=True) + norm_eps)
    grad = one * gain_ref[0:1] + two * gain_ref[1:2]

    @pl.when(pl.program_id(0) < pl.num_programs(0) // 2)
    def _():
        send_ref[0] = out
        send_ref[1] = grad

    @pl.when(pl.program_id(0) >= pl.num_programs(0) // 2)
    def _():
        keep_ref[0] = out
        keep_ref[1] = grad

    for at, value in enumerate((one * unit, one, two * unit, two)):
        norm_ref[at : at + 1] += jnp.sum(value, axis=0, keepdims=True)
    line_ref[0:1, :cut] += jnp.sum(dh_a[...].astype(f32), axis=0, keepdims=True)
    line_ref[0:1, cut:] += jnp.sum(dh_b[...].astype(f32), axis=0, keepdims=True)


def finish(tp, rowwise, weights, gains, theirs):
    length, width = rowwise[-1].shape
    block = 256
    heads = weights[0].shape[1]
    steps = length // (2 * block)
    half = steps // 2
    start = steps if theirs else 0

    def row(i, tp_ref):
        side = jnp.where(i < half, 1 - tp_ref[0], tp_ref[0])
        return start + side * half + lax.rem(i, half)

    def by_rows(value):
        return pl.BlockSpec((block, value.shape[1]), lambda i, ref: (row(i, ref), 0))

    def fixed(shape):
        return pl.BlockSpec(shape, lambda i, ref: (0, 0))

    return pl.pallas_call(
        finish_kernel,
        grid_spec=pltpu.PrefetchScalarGridSpec(
            num_scalar_prefetch=1,
            grid=(steps,),
            in_specs=[by_rows(value) for value in rowwise]
            + [fixed(value.shape) for value in weights]
            + [fixed(gains.shape)],
            out_specs=[
                pl.BlockSpec((2, block, width), lambda i, ref: (0, jnp.minimum(i, half - 1), 0)),
                pl.BlockSpec((2, block, width), lambda i, ref: (0, jnp.maximum(i - half, 0), 0)),
                fixed((4, width)),
                fixed((1, heads)),
            ],
        ),
        out_shape=[
            jax.ShapeDtypeStruct((2, half * block, width), f32),
            jax.ShapeDtypeStruct((2, half * block, width), f32),
            jax.ShapeDtypeStruct((4, width), f32),
            jax.ShapeDtypeStruct((1, heads), f32),
        ],
        compiler_params=pltpu.CompilerParams(vmem_limit_bytes=VMEM),
    )(tp, *rowwise, *weights, gains)


def after(value, *others):
    return lax.optimization_barrier((value,) + others)[0]


def gather_chunk(payload, index, widths):
    line = [swap(payload, "shard", r << 1) for r in (2, 3, 1)]
    own = jnp.stack([payload, line[2], line[0], line[1]])
    got = swap(own, "shard", 1)
    full = assemble(own, got, index, widths)
    return own, got, [value.reshape(-1, value.shape[2]) for value in full]


def adam(weight, first, second, gradient, rate, decay):
    first_new = beta_one * first + (1.0 - beta_one) * gradient
    second_new = beta_two * second + (1.0 - beta_two) * gradient * gradient
    scaled = (
        first_new
        / (1.0 - beta_one**STEP)
        / (jnp.sqrt(second_new / (1.0 - beta_two**STEP)) + adam_eps)
    )
    return (first_new, second_new, weight - rate * (scaled + decay * weight))


def adam_store(weight, first, second, gradient, outs, at):
    for ref, value in zip(outs, adam(weight[at], first[at], second[at], gradient, rate_matrix, weight_decay)):
        ref[at] = value


def adam_heads_kernel(ctx_ref, *refs):
    sums, (wq, mq, vq, wd, md, vd), outs = refs[:-12], refs[-12:-6], refs[-6:]
    pairs = len(sums) // 2
    lanes = 2 * HD
    first = ctx_ref[0] == 0
    for pair in range(pairs):
        mine, other = sums[2 * pair : 2 * pair + 2]
        for plane in range(4):
            cols = slice(plane * lanes, (plane + 1) * lanes)
            left, right = mine[:, cols], other[:, cols]
            for group, total in enumerate((jnp.where(first, left, right), jnp.where(first, right, left))):
                start = (group * pairs + pair) * lanes
                place = slice(start, start + lanes)
                if plane < 3:
                    adam_store(wq, mq, vq, total, outs[:3], (plane, slice(None), place))
                else:
                    adam_store(wd, md, vd, total.T, outs[3:], (place, slice(None)))


def adam_fc_kernel(ctx_ref, *refs):
    sums, (w1, m1, v1, w2, m2, v2), outs = refs[:-12], refs[-12:-6], refs[-6:]
    chunks = len(sums) // 2
    cut = w1.shape[1] // (2 * chunks)
    tile = 128
    first = ctx_ref[0] == 0
    for chunk in range(chunks):
        mine, other = sums[2 * chunk : 2 * chunk + 2]
        for at in range(0, 2 * cut, tile):
            left, right = mine[:, at : at + tile], other[:, at : at + tile]
            for group, total in enumerate((jnp.where(first, left, right), jnp.where(first, right, left))):
                start = (group * chunks + chunk) * cut + at % cut
                place = slice(start, start + tile)
                if at < cut:
                    adam_store(w1, m1, v1, total, outs[:3], (slice(None), place))
                else:
                    adam_store(w2, m2, v2, total.T, outs[3:], (place, slice(None)))


def adam_matrices(kernel, ctx, sums, states):
    vmem = pl.BlockSpec(memory_space=pltpu.VMEM)
    return pl.pallas_call(
        kernel,
        in_specs=[pl.BlockSpec(memory_space=pltpu.SMEM)] + [vmem] * (len(sums) + 6),
        out_specs=[vmem] * 6,
        out_shape=[jax.ShapeDtypeStruct(value.shape, f32) for value in states],
        compiler_params=pltpu.CompilerParams(vmem_limit_bytes=VMEM),
    )(ctx, *sums, *states)


def rope_tables(length, lanes):
    half = ROT // 2
    frequency = rope_base ** (-(jnp.arange(half, dtype=f32) * 2.0) / ROT)
    angle = jnp.arange(length, dtype=f32)[:, None] * frequency[None, :]
    cosine, sine = jnp.cos(angle), jnp.sin(angle)
    rest = HD - ROT
    one, none, zero = jnp.ones((length, rest), f32), jnp.zeros((length, rest), f32), jnp.zeros_like(sine)
    tables = (
        jnp.concatenate([cosine, cosine, one], axis=1),
        jnp.concatenate([-sine, zero, none], axis=1),
        jnp.concatenate([zero, sine, none], axis=1),
    )
    return [jnp.tile(table, (1, lanes // HD)) for table in tables]


def body(
    inputs, cotangent, w_qkv, m_qkv, v_qkv, w_dense, m_dense, v_dense,
    w_fc1, m_fc1, v_fc1, w_fc2, m_fc2, v_fc2, vectors, m_vectors, v_vectors,
):
    shard = lax.axis_index("shard")
    ctx = lax.axis_index("ctx")
    tp = lax.axis_index("tp")
    shards = lax.axis_size("shard")
    tok_count, width = inputs.shape
    rows = w_qkv.shape[1]
    head_cols = w_qkv.shape[2]
    units = w_fc1.shape[1]
    lanes = 2 * HD
    pairs, chunks = head_cols // (2 * lanes), 2
    own_heads, own_units = head_cols // 2, units // 2
    cut = own_units // chunks
    fc1_rows = FF // D
    count = vectors.shape[0]
    custom = shards == 8
    ctx_ref = ctx.reshape(1).astype(jnp.int32)
    shard_ref = shard.reshape(1).astype(jnp.int32)

    tp_ref = tp.reshape(1).astype(jnp.int32)
    column_ref, line_ref = shard_ref % 2, shard_ref // 2

    def gather(payload, widths):
        if custom:
            return gather_chunk(payload, shard_ref, widths)
        full = lax.all_gather(payload, "shard", axis=0, tiled=True)
        cuts = [sum(widths[:at]) for at in range(len(widths) + 1)]
        return full, full, [full[:, a:b] for a, b in zip(cuts, cuts[1:])]

    def local_grads(one, two):
        if custom:
            return grads(column_ref, normed_one if one.shape[1] == 3 * lanes else normed_two, one, all_back, two)
        first = normed_one if one.shape[1] == 3 * lanes else normed_two
        both = jnp.concatenate([dot(first, one, TN), dot(all_back, two, TN)], axis=1).astype(bf16)
        return both, both

    def step_across(kept, sent):
        if custom:
            crossed = swap(sent, "shard", 1)
            return combine(line_ref, kept, crossed)
        total = lax.psum_scatter(sent, "shard", scatter_dimension=0, tiled=True).astype(f32)
        return [total]

    def step_along(parts):
        total = parts[0]
        for r, part in zip((2, 3, 1), parts[1:]):
            total = total + swap(part, "shard", r << 1).astype(f32)
        return total, swap(total, "ctx", 1)

    with jax.named_scope("tokens"):
        part = tok_count // 2
        fetched = []

        def partner(value):
            direct = swap(pick(value.reshape(2, part, width), tp, 0), "ctx", 1)
            other = swap(direct, "tp", 1)
            fetched.append(other)
            return jnp.concatenate(
                [
                    value,
                    jnp.where(tp == 0, direct, other),
                    jnp.where(tp == 0, other, direct),
                ],
                axis=0,
            )

        all_tokens = partner(inputs)
        all_back = partner(cotangent)

    with jax.named_scope("gather_params"):
        low_qkv = pick(w_qkv.reshape(3, rows, 2, pairs, lanes), ctx, 2).astype(bf16)
        low_qkv = jnp.transpose(low_qkv, (1, 2, 0, 3)).reshape(rows, pairs * 3 * lanes)
        low_dense = pick(w_dense.reshape(2, own_heads, rows), ctx, 0).astype(bf16).T
        low_fc1 = pick(w_fc1.reshape(rows, 2, own_units), ctx, 1).astype(bf16)
        low_fc2 = pick(w_fc2.reshape(2, own_units, rows), ctx, 0).astype(bf16).T
        low_vectors = jnp.pad(vectors.astype(bf16).T, ((0, 0), (0, 128 - count)))
        payload = jnp.concatenate([low_qkv, low_dense, low_vectors], axis=1)
        _, got, (full_qkv, full_dense, full_vectors) = gather(
            payload, (pairs * 3 * lanes, pairs * lanes, 128)
        )
        full_fc1, full_fc2, lines, arrived = [], [], [], []
        gates = [got] + fetched
        for chunk in range(chunks):
            cols = slice(chunk * cut, (chunk + 1) * cut)
            payload = after(jnp.concatenate([low_fc1[:, cols], low_fc2[:, cols]], axis=1), *gates)
            own, got, (up, down) = gather(payload, (cut, cut))
            full_fc1.append(up)
            full_fc2.append(down)
            lines.append(own)
            arrived.append(got)
            gates = [own]

    vec_rows = full_vectors[:, :count].T.astype(f32)
    bias_qkv = lax.dynamic_slice_in_dim(vec_rows[0:3], tp * head_cols + ctx * own_heads, own_heads, 1)
    bias_qkv = jnp.swapaxes(bias_qkv.reshape(3, pairs, lanes), 0, 1).reshape(1, -1)
    bias_dense = vec_rows[3]
    bias_fc1 = lax.dynamic_slice_in_dim(
        vec_rows[4 : 4 + fc1_rows].reshape(1, -1), tp * units + ctx * own_units, own_units, 1
    )
    bias_fc2 = vec_rows[4 + fc1_rows]
    gain_one = vec_rows[5 + fc1_rows]
    shift_one = vec_rows[6 + fc1_rows]
    gain_two = vec_rows[7 + fc1_rows]
    shift_two = vec_rows[8 + fc1_rows]

    with jax.named_scope("norm"):
        tokens = all_tokens.astype(f32)
        centre = tokens - jnp.mean(tokens, axis=-1, keepdims=True)
        inverse = lax.rsqrt(jnp.mean(centre * centre, axis=-1, keepdims=True) + norm_eps)
        unit = centre * inverse
        normed_one = (unit * gain_one + shift_one).astype(bf16)
        normed_two = (unit * gain_two + shift_two).astype(bf16)

    tables = rope_tables(2 * tok_count, lanes)
    with jax.named_scope("project"):
        heads = (dot(normed_one, full_qkv, NN) + bias_qkv).astype(bf16)
        heads_back = dot(all_back, full_dense, NN).astype(bf16)

    def run_mlp(chunk, *gates):
        with jax.named_scope("mlp"):
            return mlp(
                normed_two, all_back, full_fc1[chunk], after(full_fc2[chunk], *gates),
                bias_fc1[:, chunk * cut : (chunk + 1) * cut],
            )

    def run_heads(pair, *gates):
        with jax.named_scope("attend"):
            return attend(ctx_ref, heads, after(heads_back, *gates), tables, pair)

    def run_finish(theirs, *gates):
        with jax.named_scope("finish"):
            rowwise = [d_heads[0], d_heads[1], attended[0], attended[1]]
            rowwise += [act[0], act[1], d_hidden[0], d_hidden[1], all_tokens]
            weights = [full_qkv, full_dense] + full_fc1 + full_fc2
            gains = after(jnp.stack([gain_one, gain_two]), *gates)
            sent, kept, norm_sums, head_line = finish(tp_ref, rowwise, weights, gains, theirs)
            return kept + swap(sent, "tp", 1), norm_sums, head_line, sent

    d_heads, attended, act, d_hidden, lines_fc1 = [], [], [], [], []

    def keep_heads(results):
        d_heads.append(results[0])
        attended.append(results[1])

    def keep_mlp(results):
        act.append(results[0])
        d_hidden.append(results[1])
        lines_fc1.append(results[2])

    keep_heads(run_heads(0, lines[0]))
    with jax.named_scope("grad_heads"):
        kept_a, sent_a = local_grads(d_heads[0], attended[0])
    keep_mlp(run_mlp(0, sent_a, lines[1]))
    with jax.named_scope("grad_fc"):
        kept_0, sent_0 = local_grads(d_hidden[0], act[0])
    with jax.named_scope("sum_heads"):
        parts_a = step_across(kept_a, sent_a)
    keep_mlp(run_mlp(1, sent_0, *parts_a))
    with jax.named_scope("grad_fc"):
        kept_1, sent_1 = local_grads(d_hidden[1], act[1])
    with jax.named_scope("sum_fc"):
        parts_0 = step_across(kept_0, sent_0)
    with jax.named_scope("sum_heads"):
        sums_a = step_along(parts_a)
    keep_heads(run_heads(1, sent_1, *parts_0, sums_a[0]))
    with jax.named_scope("sum_fc"):
        parts_1 = step_across(kept_1, sent_1)
        sums_0 = step_along(parts_0)
    theirs_sum, norm_theirs, line_theirs, sent_tp = run_finish(True, *parts_1)
    with jax.named_scope("grad_heads"):
        kept_b, sent_b = local_grads(d_heads[1], after(attended[1], sent_tp, sums_0[0]))
    with jax.named_scope("finish"):
        low_theirs = theirs_sum.astype(bf16)
    mine_sum, norm_mine, line_mine, _ = run_finish(False, low_theirs, sent_b)
    with jax.named_scope("sum_heads"):
        parts_b = step_across(kept_b, sent_b)
    with jax.named_scope("sum_fc"):
        sums_1 = step_along(parts_1)
    with jax.named_scope("sum_heads"):
        sums_b = step_along(parts_b)

    with jax.named_scope("finish"):
        norm_rows = norm_theirs + norm_mine
        head_line = line_theirs + line_mine
        total = mine_sum + swap(low_theirs, "ctx", 1).astype(f32)
        out_sum, d_unit = total[0], total[1]

        def shared(value):
            other = swap(value, "tp", 1)
            return jnp.concatenate(
                [jnp.where(tp == 0, value, other), jnp.where(tp == 0, other, value)], axis=0
            )

        own_tokens = pick(inputs.reshape(2, part, width), tp, 0).astype(f32)
        own_back = pick(cotangent.reshape(2, part, width), tp, 0).astype(f32)
        outputs = shared((own_tokens + out_sum + bias_dense + bias_fc2).astype(bf16))
        centre = own_tokens - jnp.mean(own_tokens, axis=-1, keepdims=True)
        inverse = lax.rsqrt(jnp.mean(centre * centre, axis=-1, keepdims=True) + norm_eps)
        unit = centre * inverse
        mean_d = jnp.mean(d_unit, axis=-1, keepdims=True)
        mean_du = jnp.mean(d_unit * unit, axis=-1, keepdims=True)
        input_grad = shared(own_back + inverse * (d_unit - mean_d - unit * mean_du))

    with jax.named_scope("vector_grads"):
        bias_back = jnp.sum(own_back, axis=0)[None]
        head_rows = jnp.swapaxes(head_line.reshape(pairs, 3, lanes), 0, 1).reshape(3, own_heads)
        placed_heads = lax.dynamic_update_slice_in_dim(
            jnp.zeros((3, width), f32), head_rows, tp * head_cols + ctx * own_heads, 1
        )
        placed_fc1 = lax.dynamic_update_slice_in_dim(
            jnp.zeros((1, FF), f32),
            jnp.concatenate(lines_fc1, axis=1),
            tp * units + ctx * own_units,
            1,
        ).reshape(fc1_rows, width)
        vector_grads = jnp.concatenate(
            [placed_heads, bias_back, placed_fc1, bias_back, norm_rows], axis=0
        )
        if custom:
            for axis, mask in (("tp", 1), ("shard", 1), ("shard", 2), ("ctx", 1), ("shard", 4)):
                vector_grads = vector_grads + swap(vector_grads, axis, mask)
        else:
            vector_grads = lax.psum(vector_grads, ("shard", "ctx", "tp"))
        owned_vectors = lax.dynamic_slice_in_dim(vector_grads, shard * rows, rows, 1)

    results = [outputs, input_grad]
    heads_states = (w_qkv, m_qkv, v_qkv, w_dense, m_dense, v_dense)
    fc_states = (w_fc1, m_fc1, v_fc1, w_fc2, m_fc2, v_fc2)
    head_sums = [*sums_a, *sums_b]
    fc_sums = [*sums_0, *sums_1]
    with jax.named_scope("adam"):
        if custom:
            fc_results = adam_matrices(adam_fc_kernel, ctx_ref, fc_sums, fc_states)
            results += adam_matrices(adam_heads_kernel, ctx_ref, head_sums, heads_states)
            results += fc_results
        else:

            def by_ctx(sums):
                mine, other = jnp.stack(sums[0::2]), jnp.stack(sums[1::2])
                return jnp.stack([jnp.where(ctx == 0, mine, other), jnp.where(ctx == 0, other, mine)])

            owned = by_ctx(head_sums).reshape(2, pairs, rows, 4, lanes)
            owned = jnp.transpose(owned, (3, 2, 0, 1, 4)).reshape(4, rows, head_cols)
            owned_fc = by_ctx(fc_sums).reshape(2, chunks, rows, 2, cut)
            owned_fc = jnp.transpose(owned_fc, (3, 2, 0, 1, 4)).reshape(2, rows, units)
            for gradient, entry in (
                (owned[:3], heads_states[:3]),
                (owned[3].T, heads_states[3:]),
                (owned_fc[0], fc_states[:3]),
                (owned_fc[1].T, fc_states[3:]),
            ):
                results += adam(*entry, gradient, rate_matrix, weight_decay)
        results += adam(vectors, m_vectors, v_vectors, owned_vectors, rate_vector, 0.0)
    return tuple(results)


def solution(mesh):
    tokens = P(("shard", "ctx"), None)
    layouts = [P(None, "shard", "tp"), P("tp", "shard"), P("shard", "tp"), P("tp", "shard"), P(None, "shard")]
    params = tuple(layout for layout in layouts for _ in range(3))
    return jax.shard_map(
        body,
        mesh=mesh,
        in_specs=(tokens, tokens) + params,
        out_specs=(tokens, tokens) + params,
        check_vma=False,
    )
```

time: 1430 us -> 495 us (0.35)
  waiting for transfers between devices: 738 us -> 150 us
  matrix products: 329 us -> 9.54 us
  Pallas kernels: 0 us -> 181 us
  local copies, waits for them, and re-layouts: 126 us -> 31.5 us
  other arithmetic: 141 us -> 48.6 us
  starting transfers between devices: 17.4 us -> 67.2 us
  blocking collectives: 36.5 us -> 0 us
  loops' own time: 16.5 us -> 0 us
    reduce_scatter x5 -> x0, waiting for transfers between devices: 537 us -> none  [the longest x1 152 us: body(): lax.psum_scatter(grad_fc2, 'shard', scatter_dimension=1, tiled=True)]
    dot_general x40 -> x2, matrix products: 329 us -> 9.54 us  [dot(): lax.dot_general(a, b, (contract, ((), ())), preferred_element_type=f32)]
    pallas_call x0 -> x19, Pallas kernels: none -> 181 us  [the longest x2 55.4 us: attend(): pl.pallas_call(attend_kernel, grid=(length // BQ,), in_specs=[pl.BlockSpe...]
    ppermute x0 -> x46, waiting for transfers between devices: none -> 150 us  [swap(): lax.ppermute(value, axis, [(i, i ^ mask) for i in range(lax.axis_size(axi...]
    psum x2 -> x0, waiting for transfers between devices: 89.4 us -> none  [the longest x1 82.1 us: body(): owned = lax.psum((owned[0], owned[1], owned[2], owned[3], owned[4]), 'ctx')]
    ppermute x0 -> x46, starting transfers between devices: none -> 67.2 us  [swap(): lax.ppermute(value, axis, [(i, i ^ mask) for i in range(lax.axis_size(axi...]
    all_gather x4 -> x0, waiting for transfers between devices: 66.2 us -> none  [the longest x1 56.9 us: body(): lax.all_gather(low_qkv, 'shard', axis=1, tiled=True)]
    convert_element_type x11 -> x4, other arithmetic: 65.1 us -> 7.35 us  [the longest x1 3.73 us: body(): normed_two = (unit * gain_two + shift_two).astype(bf16)]
  transfers between devices with their start and end apart: 15 -> 46, of which waited for: 11 -> 18; matrix products, arithmetic and copies ran while one was open for 39% -> 15% of each run, Pallas kernels for 0% -> 29%
where the time goes in v1:
time: 495 us; the launch traced here: 490 us
  Pallas kernels  181 us (37%)
  waiting for transfers between devices  150 us (30%)
  starting transfers between devices  67.2 us (14%)
  other arithmetic  48.6 us (10%)
  local copies, waits for them, and re-layouts  31.5 us (6%)
  matrix products  9.54 us (2%)
    ppermute x46, waiting for transfers between devices, swap(): lax.ppermute(value, axis, [(i, i ^ mask) for i in range(lax.axis_size(axi...  150 us
    ppermute x46, starting transfers between devices, swap(): lax.ppermute(value, axis, [(i, i ^ mask) for i in range(lax.axis_size(axi...  67.2 us
    pallas_call x2, Pallas kernels, attend(): pl.pallas_call(attend_kernel, grid=(length // BQ,), in_specs=[pl.BlockSpe...  55.4 us
    pallas_call x4, Pallas kernels, grads(): pl.pallas_call(grads_kernel, grid=(4,), in_specs=[pl.BlockSpec(memory_spa...  35.8 us
    pallas_call x2, Pallas kernels, finish(): pl.pallas_call(finish_kernel, grid_spec=pltpu.PrefetchScalarGridSpec(num_...  35.2 us
    pallas_call x2, Pallas kernels, mlp(): pl.pallas_call(mlp_kernel, grid=(units // UNIT_BLOCK,), in_specs=[whole,...  23.8 us
    another operation x6, local copies, waits for them, and re-layouts, rope_tables(): return [jnp.tile(table, (1, lanes // HD)) for table in tables]  14 us
    pallas_call x2, Pallas kernels, adam_matrices(): pl.pallas_call(kernel, in_specs=[pl.BlockSpec(memory_space=pltpu.SMEM)] +...  11.5 us
  transfers between devices with their start and end apart: 46, of which 18 were waited for; matrix products, arithmetic and copies ran while one was open for 15% of the time, Pallas kernels for 29%

profile of v1, /device:TPU:0, one launch (start us, length us, event | category | flops | bytes accessed | tf_op | source)
XLA Modules:
  0.0 489.8 jit_solution(13561182762939178557)
XLA Ops:
  5.0 3.0 collective-permute-start.2
  8.0 2.6 collective-permute-start.3
  10.8 1.8 collective-permute-start
  12.6 2.4 convert_reduce_fusion.2
  16.3 2.2 copy.56
  18.7 2.2 collective-permute-done.2
  20.9 10.9 %collective-permute-done.3 = bf16[128,1152]{1,0:T(8,128)(2,1)} collective-permute-done((bf16[128,1152]{1,0:T(8,128)(2,1)}, bf16[128,1152]{1,0:T(8,128)(2,1)}, u32[]{:S(2)}, u32[]{:S(2)}) %collective-permute-start.3) | collective-permute-done | bytes 294944 | tf_op jit(solution)/shard_map/gather_params/ppermute | solution.py:45
  31.8 2.3 pad_maximum_fusion.4.own_ref
  36.6 2.2 maximum_maximum_fusion.2
  38.8 19.0 %collective-permute-done.6 = bf16[512,1024]{1,0:T(8,128)(2,1)} collective-permute-done((bf16[512,1024]{1,0:T(8,128)(2,1)}, bf16[512,1024]{1,0:T(8,128)(2,1)}, u32[]{:S(2)}, u32[]{:S(2)}) %collective-permute-start.6) | collective-permute-done | bytes 1048608 | tf_op jit(solution)/shard_map/tokens/ppermute | solution.py:45
  60.4 1.8 copy.69
  62.2 2.1 tile.12
  64.4 2.5 copy.59.cos_ref
  66.9 2.2 tile.14
  69.0 2.5 copy.60.up_ref
  71.6 2.1 tile.31
  73.7 2.5 copy.61.down_ref
  78.0 3.2 gather_params.3
  83.1 3.5 collective-permute-start.9
  91.0 3.7 fusion.7
  94.7 4.8 add_convert_fusion.heads_ref
  99.5 5.7 %collective-permute-done.9 = bf16[128,1024]{1,0:T(8,128)(2,1)S(1)} collective-permute-done((bf16[128,1024]{1,0:T(8,128)(2,1)}, bf16[128,1024]{1,0:T(8,128)(2,1)S(1)}, u32[]{:S(2)}, u32[]{:S(2)}) %collective-permute-start.9) | collective-permute-done | bytes 262176 | tf_op jit(solution)/shard_map/gather_params/ppermute | solution.py:45
  105.3 5.9 %collective-permute-start.11 = (bf16[128,1024]{1,0:T(8,128)(2,1)S(1)}, bf16[128,1024]{1,0:T(8,128)(2,1)S(1)}, u32[]{:S(2)}, u32[]{:S(2)}) collective-permute-start(bf16[128,1024]{1,0:T(8,128)(2,1)S(1)} %pad_maximum_fusion.8), channel_id=1, source_target_pairs={{0,8},{4,12},{8,0},{12,4},{16,24},{20,28},{24,16},{28,20},{1,9},{5... | collective-permute-start | bytes 786440 | tf_op jit(solution)/shard_map/gather_params/ppermute | solution.py:45
  116.8 5.3 %collective-permute-done.11 = bf16[128,1024]{1,0:T(8,128)(2,1)S(1)} collective-permute-done((bf16[128,1024]{1,0:T(8,128)(2,1)S(1)}, bf16[128,1024]{1,0:T(8,128)(2,1)S(1)}, u32[]{:S(2)}, u32[]{:S(2)}) %collective-permute-start.11) | collective-permute-done | bytes 262176 | tf_op jit(solution)/shard_map/gather_params/ppermute | solution.py:45
  122.1 10.4 %collective-permute-done.12 = bf16[128,1024]{1,0:T(8,128)(2,1)S(1)} collective-permute-done((bf16[128,1024]{1,0:T(8,128)(2,1)S(1)}, bf16[128,1024]{1,0:T(8,128)(2,1)S(1)}, u32[]{:S(2)}, u32[]{:S(2)}) %collective-permute-start.12) | collective-permute-done | bytes 262176 | tf_op jit(solution)/shard_map/gather_params/ppermute | solution.py:45
  134.3 2.3 pad_maximum_fusion.1.second_ref.back_ref
  136.6 4.8 convolution_convert_fusion.back_ref
  141.3 27.5 %attend.2 = (bf16[2048,384]{1,0:T(8,128)(2,1)}, bf16[2048,128]{1,0:T(8,128)(2,1)}) custom-call(s32[1]{0:T(128)} %bitcast.3.ctx_ref, bf16[2048,768]{1,0:T(8,128)(2,1)} %add_convert_fusion.heads_ref, bf16[2048,256]{1,0:T(8,128)(2,1)} %convolution_convert_fusion.back_ref, f32[2048,128]{1,0:T(8,128)} %copy.59.cos_ref, f32[2048,128]{1,0:T(8,128)} %copy.60.up_ref, ...), custom_call_target="tpu_custom_call" | custom-call | tf_op jit(solution)/shard_map/attend/pallas_call | solution.py:198
  168.8 8.2 %grad_heads.2 = (f32[4,128,512]{2,1,0:T(8,128)}, bf16[4,128,512]{2,1,0:T(8,128)(2,1)}) custom-call(s32[1]{0:T(128)S(6)} %select_n.86.column_ref, bf16[2048,1024]{1,0:T(8,128)(2,1)} %copy-done.1, bf16[2048,384]{1,0:T(8,128)(2,1)} %get-tuple-element.92.one_ref.dh_a, bf16[2048,1024]{1,0:T(8,128)(2,1)} %pad_maximum_fusion.1.second_ref.back_ref, ...), custom_call_target="tpu_custom_call" | custom-call | tf_op jit(solution)/shard_map/grad_heads/pallas_call | solution.py:279
  178.2 9.8 %collective-permute-done.16.crossed_ref = bf16[4,128,512]{2,1,0:T(8,128)(2,1)} collective-permute-done((bf16[4,128,512]{2,1,0:T(8,128)(2,1)}, bf16[4,128,512]{2,1,0:T(8,128)(2,1)}, u32[]{:S(2)}, u32[]{:S(2)}) %collective-permute-start.16) | collective-permute-done | bytes 524320 | tf_op jit(solution)/shard_map/sum_heads/ppermute | solution.py:45
  188.0 2.3 sum_heads.2
  190.2 3.0 gather_params.5
  193.2 11.9 %mlp.2 = (bf16[2048,512]{1,0:T(8,128)(2,1)}, bf16[2048,512]{1,0:T(8,128)(2,1)}, f32[1,512]{1,0:T(1,128)}) custom-call(bf16[2048,1024]{1,0:T(8,128)(2,1)} %get-tuple-element.168.normed_ref.first_ref, bf16[2048,1024]{1,0:T(8,128)(2,1)} %pad_maximum_fusion.1.second_ref.back_ref, bf16[1024,512]{1,0:T(8,128)(2,1)} %bitcast.91, bf16[1024,512]{1,0:T(8,128)(2,1)} %bitcast.94, ...), custom_call_target="tpu_custom_call" | custom-call | tf_op jit(solution)/shard_map/mlp/pallas_call | solution.py:248
  205.1 9.7 %grad_fc.2 = (f32[4,128,1024]{2,1,0:T(8,128)}, bf16[4,128,1024]{2,1,0:T(8,128)(2,1)}) custom-call(s32[1]{0:T(128)S(6)} %select_n.86.column_ref, bf16[2048,1024]{1,0:T(8,128)(2,1)} %get-tuple-element.168.normed_ref.first_ref, bf16[2048,512]{1,0:T(8,128)(2,1)} %get-tuple-element.101.one_ref.du_a, bf16[2048,1024]{1,0:T(8,128)(2,1)} %pad_maximum_fusion.1.second_ref.back_ref, ...), custom_call_target="tpu_custom_call" | custom-call | tf_op jit(solution)/shard_map/grad_fc/pallas_call | solution.py:279
  215.3 3.0 gather_params.4
  218.3 11.9 %mlp.3 = (bf16[2048,512]{1,0:T(8,128)(2,1)}, bf16[2048,512]{1,0:T(8,128)(2,1)}, f32[1,512]{1,0:T(1,128)}) custom-call(bf16[2048,1024]{1,0:T(8,128)(2,1)} %get-tuple-element.168.normed_ref.first_ref, bf16[2048,1024]{1,0:T(8,128)(2,1)} %pad_maximum_fusion.1.second_ref.back_ref, bf16[1024,512]{1,0:T(8,128)(2,1)} %bitcast.97, bf16[1024,512]{1,0:T(8,128)(2,1)} %bitcast.100, ...), custom_call_target="tpu_custom_call" | custom-call | tf_op jit(solution)/shard_map/mlp/pallas_call | solution.py:248
  230.3 9.7 %grad_fc.3 = (f32[4,128,1024]{2,1,0:T(8,128)}, bf16[4,128,1024]{2,1,0:T(8,128)(2,1)}) custom-call(s32[1]{0:T(128)S(6)} %select_n.86.column_ref, bf16[2048,1024]{1,0:T(8,128)(2,1)} %get-tuple-element.168.normed_ref.first_ref, bf16[2048,512]{1,0:T(8,128)(2,1)} %get-tuple-element.110.one_ref.du_b, bf16[2048,1024]{1,0:T(8,128)(2,1)} %pad_maximum_fusion.1.second_ref.back_ref, ...), custom_call_target="tpu_custom_call" | custom-call | tf_op jit(solution)/shard_map/grad_fc/pallas_call | solution.py:279
  241.5 7.2 %collective-permute-start.18 = (bf16[128,512]{1,0:T(8,128)(2,1)S(1)}, bf16[128,512]{1,0:T(8,128)(2,1)S(1)}, u32[]{:S(2)}, u32[]{:S(2)}) collective-permute-start(bf16[128,512]{1,0:T(8,128)(2,1)S(1)} %copy-done.35), channel_id=1, source_target_pairs={{0,16},{4,20},{8,24},{12,28},{16,0},{20,4},{24,8},{28,12},{1,17},{... | collective-permute-start | bytes 393224 | tf_op jit(solution)/shard_map/sum_heads/ppermute | solution.py:45
  250.7 5.6 %collective-permute-done.18 = bf16[128,512]{1,0:T(8,128)(2,1)S(1)} collective-permute-done((bf16[128,512]{1,0:T(8,128)(2,1)S(1)}, bf16[128,512]{1,0:T(8,128)(2,1)S(1)}, u32[]{:S(2)}, u32[]{:S(2)}) %collective-permute-start.18) | collective-permute-done | bytes 131104 | tf_op jit(solution)/shard_map/sum_heads/ppermute | solution.py:45
  258.3 3.0 sum_fc.2
  261.3 27.9 %attend.3 = (bf16[2048,384]{1,0:T(8,128)(2,1)}, bf16[2048,128]{1,0:T(8,128)(2,1)}) custom-call(s32[1]{0:T(128)} %bitcast.3.ctx_ref, bf16[2048,768]{1,0:T(8,128)(2,1)} %add_convert_fusion.heads_ref, bf16[2048,256]{1,0:T(8,128)(2,1)} %convolution_convert_fusion.back_ref, f32[2048,128]{1,0:T(8,128)} %copy.59.cos_ref, f32[2048,128]{1,0:T(8,128)} %copy.60.up_ref, ...), custom_call_target="tpu_custom_call" | custom-call | tf_op jit(solution)/shard_map/attend/pallas_call | solution.py:198
  290.2 3.0 sum_fc.3
  293.3 17.5 %finish.2 = (f32[2,512,1024]{2,1,0:T(8,128)}, f32[2,512,1024]{2,1,0:T(8,128)}, f32[4,1024]{1,0:T(4,128)}, f32[1,768]{1,0:T(1,128)}) custom-call(s32[1]{0:T(128)} %bitcast.2.tp_ref, bf16[2048,384]{1,0:T(8,128)(2,1)} %get-tuple-element.92.one_ref.dh_a, bf16[2048,384]{1,0:T(8,128)(2,1)} %get-tuple-element.119.dh_b.one_ref, ...), custom_call_target="tpu_custom_call" | custom-call | tf_op jit(solution)/shard_map/finish/pallas_call | solution.py:374
  312.0 2.4 collective-permute-start.24
  314.4 17.8 %collective-permute-done.23 = bf16[128,1024]{1,0:T(8,128)(2,1)S(1)} collective-permute-done((bf16[128,1024]{1,0:T(8,128)(2,1)S(1)}, bf16[128,1024]{1,0:T(8,128)(2,1)S(1)}, u32[]{:S(2)}, u32[]{:S(2)}) %collective-permute-start.23) | collective-permute-done | bytes 262176 | tf_op jit(solution)/shard_map/sum_fc/ppermute | solution.py:45
  334.0 8.1 %grad_heads.3 = (f32[4,128,512]{2,1,0:T(8,128)}, bf16[4,128,512]{2,1,0:T(8,128)(2,1)}) custom-call(s32[1]{0:T(128)S(6)} %select_n.86.column_ref, bf16[2048,1024]{1,0:T(8,128)(2,1)} %copy-done.1, bf16[2048,384]{1,0:T(8,128)(2,1)} %get-tuple-element.119.dh_b.one_ref, bf16[2048,1024]{1,0:T(8,128)(2,1)} %pad_maximum_fusion.1.second_ref.back_ref, ...), custom_call_target="tpu_custom_call" | custom-call | tf_op jit(solution)/shard_map/grad_heads/pallas_call | solution.py:279
  342.2 2.9 add_convert_fusion.1
  345.1 17.6 %finish.3 = (f32[2,512,1024]{2,1,0:T(8,128)}, f32[2,512,1024]{2,1,0:T(8,128)}, f32[4,1024]{1,0:T(4,128)}, f32[1,768]{1,0:T(1,128)}) custom-call(s32[1]{0:T(128)} %bitcast.2.tp_ref, bf16[2048,384]{1,0:T(8,128)(2,1)} %get-tuple-element.92.one_ref.dh_a, bf16[2048,384]{1,0:T(8,128)(2,1)} %get-tuple-element.119.dh_b.one_ref, ...), custom_call_target="tpu_custom_call" | custom-call | tf_op jit(solution)/shard_map/finish/pallas_call | solution.py:374
  366.1 5.3 %collective-permute-start.37 = (bf16[128,1024]{1,0:T(8,128)(2,1)}, bf16[128,1024]{1,0:T(8,128)(2,1)}, u32[]{:S(2)}, u32[]{:S(2)}) collective-permute-start(bf16[128,1024]{1,0:T(8,128)(2,1)} %get-tuple-element.123), channel_id=1, source_target_pairs={{0,16},{4,20},{8,24},{12,28},{16,0},{20,4},{24,8},{28,12},{1,17},{... | collective-permute-start | bytes 786440 | tf_op jit(solution)/shard_map/sum_fc/ppermute | solution.py:45
  372.8 38.2 %collective-permute-done.27 = bf16[2,512,1024]{2,1,0:T(8,128)(2,1)} collective-permute-done((bf16[2,512,1024]{2,1,0:T(8,128)(2,1)S(1)}, bf16[2,512,1024]{2,1,0:T(8,128)(2,1)}, u32[]{:S(2)}, u32[]{:S(2)}) %collective-permute-start.27) | collective-permute-done | bytes 2097184 | tf_op jit(solution)/shard_map/finish/ppermute | solution.py:45
  411.0 5.7 %convert_add_fusion = f32[2,512,1024]{2,1,0:T(8,128)S(1)} fusion(bf16[2,512,1024]{2,1,0:T(8,128)(2,1)} %collective-permute-done.27, f32[2,512,1024]{2,1,0:T(8,128)} %get-tuple-element.132, f32[2,512,1024]{2,1,0:T(8,128)} %collective-permute-done.26), kind=kLoop, calls=%fused_computation.15 | loop fusion | flops 3145728 | bytes 14680064 | tf_op jit(solution)/shard_map/finish/add | solution.py:678
  417.4 3.1 convert_add_fusion.2
  421.2 1.9 collective-permute-start.38
  424.5 4.9 collective-permute-start.39
  430.0 2.3 sum_heads.3
  433.7 1.9 collective-permute-start.33
  437.3 2.0 collective-permute-start.34
  439.3 6.4 %collective-permute-done.32 = bf16[128,512]{1,0:T(8,128)(2,1)S(1)} collective-permute-done((bf16[128,512]{1,0:T(8,128)(2,1)}, bf16[128,512]{1,0:T(8,128)(2,1)S(1)}, u32[]{:S(2)}, u32[]{:S(2)}) %collective-permute-start.32) | collective-permute-done | bytes 131104 | tf_op jit(solution)/shard_map/sum_heads/ppermute | solution.py:45
  447.0 3.0 collective-permute-done.43
  454.7 11.5 %collective-permute-done.44 = f32[13,1024]{1,0:T(8,128)S(1)} collective-permute-done((f32[13,1024]{1,0:T(8,128)S(1)}, f32[13,1024]{1,0:T(8,128)S(1)}, u32[]{:S(2)}, u32[]{:S(2)}) %collective-permute-start.44) | collective-permute-done | bytes 53280 | tf_op jit(solution)/shard_map/vector_grads/ppermute | solution.py:45
  469.2 7.0 %adam.3 = (f32[128,2048]{1,0:T(8,128)}, f32[128,2048]{1,0:T(8,128)}, f32[128,2048]{1,0:T(8,128)}, f32[2048,128]{1,0:T(8,128)}, f32[2048,128]{1,0:T(8,128)}, /*index=5*/f32[2048,128]{1,0:T(8,128)}) custom-call(s32[1]{0:T(128)} %bitcast.3.ctx_ref, f32[128,1024]{1,0:T(8,128)} %convert_add_fusion.4.refs_0_, f32[128,1024]{1,0:T(8,128)} %copy-done.17, ...), custom_call_target="tpu_custom_call" | custom-call | tf_op jit(solution)/shard_map/adam/pallas_call | solution.py:467
  476.9 4.5 adam.2
  485.0 2.0 broadcast_select_fusion.1
  487.1 2.5 pad_maximum_fusion.2
  (209 shorter events, 62.0 us)
Async XLA Ops:
  5.0 15.9 %collective-permute-start.2 = (bf16[128,1152]{1,0:T(8,128)(2,1)}, bf16[128,1152]{1,0:T(8,128)(2,1)}, u32[]{:S(2)}, u32[]{:S(2)}) collective-permute-start(bf16[128,1152]{1,0:T(8,128)(2,1)} %get-tuple-element.179), channel_id=1, source_target_pairs={{0,8},{4,12},{8,0},{12,4},{16,24},{20,28},{24,16},{28,20},{1,9},{5... | collective-permute-start | bytes 884744 | tf_op jit(solution)/shard_map/gather_params/ppermute | solution.py:45
  8.0 23.8 %collective-permute-start.3 = (bf16[128,1152]{1,0:T(8,128)(2,1)}, bf16[128,1152]{1,0:T(8,128)(2,1)}, u32[]{:S(2)}, u32[]{:S(2)}) collective-permute-start(bf16[128,1152]{1,0:T(8,128)(2,1)} %get-tuple-element.179), channel_id=1, source_target_pairs={{0,16},{4,20},{8,24},{12,28},{16,0},{20,4},{24,8},{28,12},{1,17},{... | collective-permute-start | bytes 884744 | tf_op jit(solution)/shard_map/gather_params/ppermute | solution.py:45
  10.6 21.2 %collective-permute-start.4 = (bf16[128,1152]{1,0:T(8,128)(2,1)}, bf16[128,1152]{1,0:T(8,128)(2,1)}, u32[]{:S(2)}, u32[]{:S(2)}) collective-permute-start(bf16[128,1152]{1,0:T(8,128)(2,1)} %get-tuple-element.179), channel_id=1, source_target_pairs={{0,24},{4,28},{8,16},{12,20},{16,8},{20,12},{24,0},{28,4},{1,25},{... | collective-permute-start | bytes 884744 | tf_op jit(solution)/shard_map/gather_params/ppermute | solution.py:45
  10.8 28.0 %collective-permute-start = (bf16[512,1024]{1,0:T(8,128)(2,1)S(1)}, bf16[512,1024]{1,0:T(8,128)(2,1)}, u32[]{:S(2)}, u32[]{:S(2)}) collective-permute-start(bf16[512,1024]{1,0:T(8,128)(2,1)S(1)} %get-tuple-element.163), channel_id=1, source_target_pairs={{0,2},{2,0},{1,3},{3,1},{4,6},{6,4},{5,7},{7,5},{8,10},{10,8},{9,1... | collective-permute-start | bytes 3145736 | tf_op jit(solution)/shard_map/tokens/ppermute | solution.py:45
  15.0 42.8 %collective-permute-start.6 = (bf16[512,1024]{1,0:T(8,128)(2,1)}, bf16[512,1024]{1,0:T(8,128)(2,1)}, u32[]{:S(2)}, u32[]{:S(2)}) collective-permute-start(bf16[512,1024]{1,0:T(8,128)(2,1)} %get-tuple-element.161), channel_id=1, source_target_pairs={{0,2},{2,0},{1,3},{3,1},{4,6},{6,4},{5,7},{7,5},{8,10},{10,8},{9,1... | collective-permute-start | bytes 3145736 | tf_op jit(solution)/shard_map/tokens/ppermute | solution.py:45
  34.2 43.8 %collective-permute-start.5 = (bf16[4,128,1152]{2,1,0:T(8,128)(2,1)}, bf16[4,128,1152]{2,1,0:T(8,128)(2,1)}, u32[]{:S(2)}, u32[]{:S(2)}) collective-permute-start(bf16[4,128,1152]{2,1,0:T(8,128)(2,1)} %pad_maximum_fusion.4.own_ref), channel_id=1, source_target_pairs={{0,4},{4,0},{8,12},{12,8},{16,20},{20,16},{24,28},{28,24},{1,5},{5... | collective-permute-start | bytes 3538952 | tf_op jit(solution)/shard_map/gather_params/ppermute | solution.py:45
  38.8 43.5 %collective-permute-start.1 = (bf16[512,1024]{1,0:T(8,128)(2,1)}, bf16[512,1024]{1,0:T(8,128)(2,1)}, u32[]{:S(2)}, u32[]{:S(2)}) collective-permute-start(bf16[512,1024]{1,0:T(8,128)(2,1)} %collective-permute-done), channel_id=1, source_target_pairs={{0,1},{1,0},{2,3},{3,2},{4,5},{5,4},{6,7},{7,6},{8,9},{9,8},{10,11... | collective-permute-start | bytes 3145736 | tf_op jit(solution)/shard_map/tokens/ppermute | solution.py:45
  57.8 24.5 %collective-permute-start.7 = (bf16[512,1024]{1,0:T(8,128)(2,1)}, bf16[512,1024]{1,0:T(8,128)(2,1)}, u32[]{:S(2)}, u32[]{:S(2)}) collective-permute-start(bf16[512,1024]{1,0:T(8,128)(2,1)} %collective-permute-done.6), channel_id=1, source_target_pairs={{0,1},{1,0},{2,3},{3,2},{4,5},{5,4},{6,7},{7,6},{8,9},{9,8},{10,11... | collective-permute-start | bytes 3145736 | tf_op jit(solution)/shard_map/tokens/ppermute | solution.py:45
  82.4 17.1 %collective-permute-start.8 = (bf16[128,1024]{1,0:T(8,128)(2,1)}, bf16[128,1024]{1,0:T(8,128)(2,1)S(1)}, u32[]{:S(2)}, u32[]{:S(2)}) collective-permute-start(bf16[128,1024]{1,0:T(8,128)(2,1)} %pad_maximum_fusion.7), channel_id=1, source_target_pairs={{0,8},{4,12},{8,0},{12,4},{16,24},{20,28},{24,16},{28,20},{1,9},{5... | collective-permute-start | bytes 786440 | tf_op jit(solution)/shard_map/gather_params/ppermute | solution.py:45
  83.1 22.1 %collective-permute-start.9 = (bf16[128,1024]{1,0:T(8,128)(2,1)}, bf16[128,1024]{1,0:T(8,128)(2,1)S(1)}, u32[]{:S(2)}, u32[]{:S(2)}) collective-permute-start(bf16[128,1024]{1,0:T(8,128)(2,1)} %pad_maximum_fusion.7), channel_id=1, source_target_pairs={{0,16},{4,20},{8,24},{12,28},{16,0},{20,4},{24,8},{28,12},{1,17},{... | collective-permute-start | bytes 786440 | tf_op jit(solution)/shard_map/gather_params/ppermute | solution.py:45
  86.5 18.6 %collective-permute-start.10 = (bf16[128,1024]{1,0:T(8,128)(2,1)}, bf16[128,1024]{1,0:T(8,128)(2,1)S(1)}, u32[]{:S(2)}, u32[]{:S(2)}) collective-permute-start(bf16[128,1024]{1,0:T(8,128)(2,1)} %pad_maximum_fusion.7), channel_id=1, source_target_pairs={{0,24},{4,28},{8,16},{12,20},{16,8},{20,12},{24,0},{28,4},{1,25},{... | collective-permute-start | bytes 786440 | tf_op jit(solution)/shard_map/gather_params/ppermute | solution.py:45
  94.7 10.4 %copy-start.16 = (bf16[128,1024]{1,0:T(8,128)(2,1)S(1)}, bf16[128,1024]{1,0:T(8,128)(2,1)}, u32[]{:S(2)}) copy-start(bf16[128,1024]{1,0:T(8,128)(2,1)} %pad_maximum_fusion.7) | copy-start | bytes 786436
  105.2 29.1 %copy-start.4 = (bf16[1024,1024]{1,0:T(8,128)(2,1)S(1)}, bf16[1024,1024]{1,0:T(8,128)(2,1)}, u32[]{:S(2)}) copy-start(bf16[1024,1024]{1,0:T(8,128)(2,1)} %param.18) | copy-start | bytes 6291460
  105.3 31.3 %copy-start.6 = (bf16[4,128,1024]{2,1,0:T(8,128)(2,1)}, bf16[4,128,1024]{2,1,0:T(8,128)(2,1)S(1)}, u32[]{:S(2)}) copy-start(bf16[4,128,1024]{2,1,0:T(8,128)(2,1)S(1)} %pad_maximum_fusion.5.own_ref) | copy-start | bytes 3145732
  105.3 16.8 %collective-permute-start.11 = (bf16[128,1024]{1,0:T(8,128)(2,1)S(1)}, bf16[128,1024]{1,0:T(8,128)(2,1)S(1)}, u32[]{:S(2)}, u32[]{:S(2)}) collective-permute-start(bf16[128,1024]{1,0:T(8,128)(2,1)S(1)} %pad_maximum_fusion.8), channel_id=1, source_target_pairs={{0,8},{4,12},{8,0},{12,4},{16,24},{20,28},{24,16},{28,20},{1,9},{5... | collective-permute-start | bytes 786440 | tf_op jit(solution)/shard_map/gather_params/ppermute | solution.py:45
  111.2 21.4 %collective-permute-start.12 = (bf16[128,1024]{1,0:T(8,128)(2,1)S(1)}, bf16[128,1024]{1,0:T(8,128)(2,1)S(1)}, u32[]{:S(2)}, u32[]{:S(2)}) collective-permute-start(bf16[128,1024]{1,0:T(8,128)(2,1)S(1)} %pad_maximum_fusion.8), channel_id=1, source_target_pairs={{0,16},{4,20},{8,24},{12,28},{16,0},{20,4},{24,8},{28,12},{1,17},{... | collective-permute-start | bytes 786440 | tf_op jit(solution)/shard_map/gather_params/ppermute | solution.py:45
  112.2 20.4 %collective-permute-start.13 = (bf16[128,1024]{1,0:T(8,128)(2,1)S(1)}, bf16[128,1024]{1,0:T(8,128)(2,1)S(1)}, u32[]{:S(2)}, u32[]{:S(2)}) collective-permute-start(bf16[128,1024]{1,0:T(8,128)(2,1)S(1)} %pad_maximum_fusion.8), channel_id=1, source_target_pairs={{0,24},{4,28},{8,16},{12,20},{16,8},{20,12},{24,0},{28,4},{1,25},{... | collective-permute-start | bytes 786440 | tf_op jit(solution)/shard_map/gather_params/ppermute | solution.py:45
  115.3 74.9 %collective-permute-start.15 = (bf16[4,128,1024]{2,1,0:T(8,128)(2,1)S(1)}, bf16[4,128,1024]{2,1,0:T(8,128)(2,1)}, u32[]{:S(2)}, u32[]{:S(2)}) collective-permute-start(bf16[4,128,1024]{2,1,0:T(8,128)(2,1)S(1)} %pad_maximum_fusion.5.own_ref), channel_id=1, source_target_pairs={{0,4},{4,0},{8,12},{12,8},{16,20},{20,16},{24,28},{28,24},{1,5},{5... | collective-permute-start | bytes 3145736 | tf_op jit(solution)/shard_map/gather_params/ppermute | solution.py:45
  132.7 82.6 %collective-permute-start.14 = (bf16[4,128,1024]{2,1,0:T(8,128)(2,1)S(1)}, bf16[4,128,1024]{2,1,0:T(8,128)(2,1)}, u32[]{:S(2)}, u32[]{:S(2)}) collective-permute-start(bf16[4,128,1024]{2,1,0:T(8,128)(2,1)S(1)} %pad_maximum_fusion.6.own_ref), channel_id=1, source_target_pairs={{0,4},{4,0},{8,12},{12,8},{16,20},{20,16},{24,28},{28,24},{1,5},{5... | collective-permute-start | bytes 3145736 | tf_op jit(solution)/shard_map/gather_params/ppermute | solution.py:45
  177.0 10.9 %collective-permute-start.16 = (bf16[4,128,512]{2,1,0:T(8,128)(2,1)}, bf16[4,128,512]{2,1,0:T(8,128)(2,1)}, u32[]{:S(2)}, u32[]{:S(2)}) collective-permute-start(bf16[4,128,512]{2,1,0:T(8,128)(2,1)} %get-tuple-element.99), channel_id=1, source_target_pairs={{0,4},{4,0},{8,12},{12,8},{16,20},{20,16},{24,28},{28,24},{1,5},{5... | collective-permute-start | bytes 1572872 | tf_op jit(solution)/shard_map/sum_heads/ppermute | solution.py:45
  214.8 42.5 %collective-permute-start.17 = (bf16[4,128,1024]{2,1,0:T(8,128)(2,1)}, bf16[4,128,1024]{2,1,0:T(8,128)(2,1)S(1)}, u32[]{:S(2)}, u32[]{:S(2)}) collective-permute-start(bf16[4,128,1024]{2,1,0:T(8,128)(2,1)} %get-tuple-element.103), channel_id=1, source_target_pairs={{0,4},{4,0},{8,12},{12,8},{16,20},{20,16},{24,28},{28,24},{1,5},{5... | collective-permute-start | bytes 3145736 | tf_op jit(solution)/shard_map/sum_fc/ppermute | solution.py:45
  230.2 11.2 %copy-start.35 = (bf16[128,512]{1,0:T(8,128)(2,1)S(1)}, bf16[128,512]{1,0:T(8,128)(2,1)}, u32[]{:S(2)}) copy-start(bf16[128,512]{1,0:T(8,128)(2,1)} %get-tuple-element.106) | copy-start | bytes 393220
  230.2 18.4 %copy-start.34 = (bf16[128,512]{1,0:T(8,128)(2,1)S(1)}, bf16[128,512]{1,0:T(8,128)(2,1)}, u32[]{:S(2)}) copy-start(bf16[128,512]{1,0:T(8,128)(2,1)} %get-tuple-element.107) | copy-start | bytes 393220
  230.3 19.9 %copy-start.33 = (bf16[128,512]{1,0:T(8,128)(2,1)S(1)}, bf16[128,512]{1,0:T(8,128)(2,1)}, u32[]{:S(2)}) copy-start(bf16[128,512]{1,0:T(8,128)(2,1)} %get-tuple-element.108) | copy-start | bytes 393220
  230.3 26.9 %copy-start.20 = (f32[128,512]{1,0:T(8,128)S(1)}, f32[128,512]{1,0:T(8,128)}, u32[]{:S(2)}) copy-start(f32[128,512]{1,0:T(8,128)} %get-tuple-element.105) | copy-start | bytes 786436
  240.0 49.2 %collective-permute-start.21 = (bf16[4,128,1024]{2,1,0:T(8,128)(2,1)}, bf16[4,128,1024]{2,1,0:T(8,128)(2,1)S(1)}, u32[]{:S(2)}, u32[]{:S(2)}) collective-permute-start(bf16[4,128,1024]{2,1,0:T(8,128)(2,1)} %get-tuple-element.112), channel_id=1, source_target_pairs={{0,4},{4,0},{8,12},{12,8},{16,20},{20,16},{24,28},{28,24},{1,5},{5... | collective-permute-start | bytes 3145736 | tf_op jit(solution)/shard_map/sum_fc/ppermute | solution.py:45
  241.5 14.9 %collective-permute-start.18 = (bf16[128,512]{1,0:T(8,128)(2,1)S(1)}, bf16[128,512]{1,0:T(8,128)(2,1)S(1)}, u32[]{:S(2)}, u32[]{:S(2)}) collective-permute-start(bf16[128,512]{1,0:T(8,128)(2,1)S(1)} %copy-done.35), channel_id=1, source_target_pairs={{0,16},{4,20},{8,24},{12,28},{16,0},{20,4},{24,8},{28,12},{1,17},{... | collective-permute-start | bytes 393224 | tf_op jit(solution)/shard_map/sum_heads/ppermute | solution.py:45
  248.7 7.7 %collective-permute-start.19 = (bf16[128,512]{1,0:T(8,128)(2,1)S(1)}, bf16[128,512]{1,0:T(8,128)(2,1)S(1)}, u32[]{:S(2)}, u32[]{:S(2)}) collective-permute-start(bf16[128,512]{1,0:T(8,128)(2,1)S(1)} %copy-done.34), channel_id=1, source_target_pairs={{0,24},{4,28},{8,16},{12,20},{16,8},{20,12},{24,0},{28,4},{1,25},{... | collective-permute-start | bytes 393224 | tf_op jit(solution)/shard_map/sum_heads/ppermute | solution.py:45
  250.1 7.1 %collective-permute-start.20 = (bf16[128,512]{1,0:T(8,128)(2,1)S(1)}, bf16[128,512]{1,0:T(8,128)(2,1)S(1)}, u32[]{:S(2)}, u32[]{:S(2)}) collective-permute-start(bf16[128,512]{1,0:T(8,128)(2,1)S(1)} %copy-done.33), channel_id=1, source_target_pairs={{0,8},{4,12},{8,0},{12,4},{16,24},{20,28},{24,16},{28,20},{1,9},{5... | collective-permute-start | bytes 393224 | tf_op jit(solution)/shard_map/sum_heads/ppermute | solution.py:45
  257.3 195.9 %copy-start.11 = (f32[128,512]{1,0:T(8,128)}, f32[128,512]{1,0:T(8,128)S(1)}, u32[]{:S(2)}) copy-start(f32[128,512]{1,0:T(8,128)S(1)} %convert_add_fusion.6.refs_0_) | copy-start | bytes 786436
  293.3 17.6 %copy-start.32 = (bf16[128,1024]{1,0:T(8,128)(2,1)S(1)}, bf16[128,1024]{1,0:T(8,128)(2,1)}, u32[]{:S(2)}) copy-start(bf16[128,1024]{1,0:T(8,128)(2,1)} %get-tuple-element.115) | copy-start | bytes 786436
  293.3 18.7 %copy-start.31 = (bf16[128,1024]{1,0:T(8,128)(2,1)S(1)}, bf16[128,1024]{1,0:T(8,128)(2,1)}, u32[]{:S(2)}) copy-start(bf16[128,1024]{1,0:T(8,128)(2,1)} %get-tuple-element.116) | copy-start | bytes 786436
  293.3 21.1 %copy-start.30 = (bf16[128,1024]{1,0:T(8,128)(2,1)S(1)}, bf16[128,1024]{1,0:T(8,128)(2,1)}, u32[]{:S(2)}) copy-start(bf16[128,1024]{1,0:T(8,128)(2,1)} %get-tuple-element.117) | copy-start | bytes 786436
  293.3 39.8 %copy-start.19 = (f32[128,1024]{1,0:T(8,128)S(1)}, f32[128,1024]{1,0:T(8,128)}, u32[]{:S(2)}) copy-start(f32[128,1024]{1,0:T(8,128)} %get-tuple-element.114) | copy-start | bytes 1572868
  310.8 31.4 %collective-permute-start.22 = (f32[2,512,1024]{2,1,0:T(8,128)}, f32[2,512,1024]{2,1,0:T(8,128)}, u32[]{:S(2)}, u32[]{:S(2)}) collective-permute-start(f32[2,512,1024]{2,1,0:T(8,128)} %get-tuple-element.128), channel_id=1, source_target_pairs={{0,1},{1,0},{2,3},{3,2},{4,5},{5,4},{6,7},{7,6},{8,9},{9,8},{10,11... | collective-permute-start | bytes 12582920 | tf_op jit(solution)/shard_map/finish/ppermute | solution.py:45
  310.9 21.4 %collective-permute-start.23 = (bf16[128,1024]{1,0:T(8,128)(2,1)S(1)}, bf16[128,1024]{1,0:T(8,128)(2,1)S(1)}, u32[]{:S(2)}, u32[]{:S(2)}) collective-permute-start(bf16[128,1024]{1,0:T(8,128)(2,1)S(1)} %copy-done.32), channel_id=1, source_target_pairs={{0,16},{4,20},{8,24},{12,28},{16,0},{20,4},{24,8},{28,12},{1,17},{... | collective-permute-start | bytes 786440 | tf_op jit(solution)/shard_map/sum_fc/ppermute | solution.py:45
  312.0 20.2 %collective-permute-start.24 = (bf16[128,1024]{1,0:T(8,128)(2,1)S(1)}, bf16[128,1024]{1,0:T(8,128)(2,1)S(1)}, u32[]{:S(2)}, u32[]{:S(2)}) collective-permute-start(bf16[128,1024]{1,0:T(8,128)(2,1)S(1)} %copy-done.31), channel_id=1, source_target_pairs={{0,24},{4,28},{8,16},{12,20},{16,8},{20,12},{24,0},{28,4},{1,25},{... | collective-permute-start | bytes 786440 | tf_op jit(solution)/shard_map/sum_fc/ppermute | solution.py:45
  314.4 18.7 %collective-permute-start.25 = (bf16[128,1024]{1,0:T(8,128)(2,1)S(1)}, bf16[128,1024]{1,0:T(8,128)(2,1)S(1)}, u32[]{:S(2)}, u32[]{:S(2)}) collective-permute-start(bf16[128,1024]{1,0:T(8,128)(2,1)S(1)} %copy-done.30), channel_id=1, source_target_pairs={{0,8},{4,12},{8,0},{12,4},{16,24},{20,28},{24,16},{28,20},{1,9},{5... | collective-permute-start | bytes 786440 | tf_op jit(solution)/shard_map/sum_fc/ppermute | solution.py:45
  345.1 19.8 %copy-start.28 = (f32[1,512]{1,0:T(1,128)S(1)}, f32[1,512]{1,0:T(1,128)}, u32[]{:S(2)}) copy-start(f32[1,512]{1,0:T(1,128)} %get-tuple-element.153) | copy-start | bytes 6148
  345.1 19.8 %copy-start.29 = (f32[1,512]{1,0:T(1,128)S(1)}, f32[1,512]{1,0:T(1,128)}, u32[]{:S(2)}) copy-start(f32[1,512]{1,0:T(1,128)} %get-tuple-element.154) | copy-start | bytes 6148
  345.1 27.0 %copy-start.27 = (f32[1,768]{1,0:T(1,128)S(1)}, f32[1,768]{1,0:T(1,128)}, u32[]{:S(2)}) copy-start(f32[1,768]{1,0:T(1,128)} %get-tuple-element.151) | copy-start | bytes 9220
  362.8 48.2 %collective-permute-start.26 = (f32[2,512,1024]{2,1,0:T(8,128)}, f32[2,512,1024]{2,1,0:T(8,128)}, u32[]{:S(2)}, u32[]{:S(2)}) collective-permute-start(f32[2,512,1024]{2,1,0:T(8,128)} %get-tuple-element.133), channel_id=1, source_target_pairs={{0,1},{1,0},{2,3},{3,2},{4,5},{5,4},{6,7},{7,6},{8,9},{9,8},{10,11... | collective-permute-start | bytes 12582920 | tf_op jit(solution)/shard_map/finish/ppermute | solution.py:45
  362.8 48.1 %collective-permute-start.27 = (bf16[2,512,1024]{2,1,0:T(8,128)(2,1)S(1)}, bf16[2,512,1024]{2,1,0:T(8,128)(2,1)}, u32[]{:S(2)}, u32[]{:S(2)}) collective-permute-start(bf16[2,512,1024]{2,1,0:T(8,128)(2,1)S(1)} %add_convert_fusion.1), channel_id=1, source_target_pairs={{0,2},{2,0},{1,3},{3,1},{4,6},{6,4},{5,7},{7,5},{8,10},{10,8},{9,1... | collective-permute-start | bytes 6291464 | tf_op jit(solution)/shard_map/finish/ppermute | solution.py:45
  366.1 66.1 %collective-permute-start.37 = (bf16[128,1024]{1,0:T(8,128)(2,1)}, bf16[128,1024]{1,0:T(8,128)(2,1)}, u32[]{:S(2)}, u32[]{:S(2)}) collective-permute-start(bf16[128,1024]{1,0:T(8,128)(2,1)} %get-tuple-element.123), channel_id=1, source_target_pairs={{0,16},{4,20},{8,24},{12,28},{16,0},{20,4},{24,8},{28,12},{1,17},{... | collective-permute-start | bytes 786440 | tf_op jit(solution)/shard_map/sum_fc/ppermute | solution.py:45
  371.4 57.9 %collective-permute-start.31 = (bf16[4,128,512]{2,1,0:T(8,128)(2,1)}, bf16[4,128,512]{2,1,0:T(8,128)(2,1)}, u32[]{:S(2)}, u32[]{:S(2)}) collective-permute-start(bf16[4,128,512]{2,1,0:T(8,128)(2,1)} %get-tuple-element.130), channel_id=1, source_target_pairs={{0,4},{4,0},{8,12},{12,8},{16,20},{20,16},{24,28},{28,24},{1,5},{5... | collective-permute-start | bytes 1572872 | tf_op jit(solution)/shard_map/sum_heads/ppermute | solution.py:45
  420.5 64.5 %collective-permute-start.29 = (f32[512,1024]{1,0:T(8,128)S(1)}, f32[512,1024]{1,0:T(8,128)}, u32[]{:S(2)}, u32[]{:S(2)}) collective-permute-start(f32[512,1024]{1,0:T(8,128)S(1)} %get-tuple-element.166), channel_id=1, source_target_pairs={{0,1},{1,0},{2,3},{3,2},{4,5},{5,4},{6,7},{7,6},{8,9},{9,8},{10,11... | collective-permute-start | bytes 6291464 | tf_op jit(solution)/shard_map/finish/ppermute | solution.py:45
  420.7 3.8 collective-permute-start.41
  421.2 14.4 %collective-permute-start.38 = (bf16[128,1024]{1,0:T(8,128)(2,1)}, bf16[128,1024]{1,0:T(8,128)(2,1)S(1)}, u32[]{:S(2)}, u32[]{:S(2)}) collective-permute-start(bf16[128,1024]{1,0:T(8,128)(2,1)} %get-tuple-element.124), channel_id=1, source_target_pairs={{0,24},{4,28},{8,16},{12,20},{16,8},{20,12},{24,0},{28,4},{1,25},{... | collective-permute-start | bytes 786440 | tf_op jit(solution)/shard_map/sum_fc/ppermute | solution.py:45
  424.5 12.9 %collective-permute-start.39 = (bf16[128,1024]{1,0:T(8,128)(2,1)}, bf16[128,1024]{1,0:T(8,128)(2,1)S(1)}, u32[]{:S(2)}, u32[]{:S(2)}) collective-permute-start(bf16[128,1024]{1,0:T(8,128)(2,1)} %get-tuple-element.125), channel_id=1, source_target_pairs={{0,8},{4,12},{8,0},{12,4},{16,24},{20,28},{24,16},{28,20},{1,9},{5... | collective-permute-start | bytes 786440 | tf_op jit(solution)/shard_map/sum_fc/ppermute | solution.py:45
  429.4 4.3 collective-permute-start.42
  432.2 13.5 %collective-permute-start.32 = (bf16[128,512]{1,0:T(8,128)(2,1)}, bf16[128,512]{1,0:T(8,128)(2,1)S(1)}, u32[]{:S(2)}, u32[]{:S(2)}) collective-permute-start(bf16[128,512]{1,0:T(8,128)(2,1)} %get-tuple-element.136), channel_id=1, source_target_pairs={{0,16},{4,20},{8,24},{12,28},{16,0},{20,4},{24,8},{28,12},{1,17},{... | collective-permute-start | bytes 393224 | tf_op jit(solution)/shard_map/sum_heads/ppermute | solution.py:45
  433.7 12.0 %collective-permute-start.33 = (bf16[128,512]{1,0:T(8,128)(2,1)}, bf16[128,512]{1,0:T(8,128)(2,1)S(1)}, u32[]{:S(2)}, u32[]{:S(2)}) collective-permute-start(bf16[128,512]{1,0:T(8,128)(2,1)} %get-tuple-element.137), channel_id=1, source_target_pairs={{0,24},{4,28},{8,16},{12,20},{16,8},{20,12},{24,0},{28,4},{1,25},{... | collective-permute-start | bytes 393224 | tf_op jit(solution)/shard_map/sum_heads/ppermute | solution.py:45
  435.6 17.5 %collective-permute-start.36 = (f32[128,1024]{1,0:T(8,128)}, f32[128,1024]{1,0:T(8,128)S(1)}, u32[]{:S(2)}, u32[]{:S(2)}) collective-permute-start(f32[128,1024]{1,0:T(8,128)} %convert_add_fusion.4.refs_0_), channel_id=1, source_target_pairs={{0,2},{2,0},{1,3},{3,1},{4,6},{6,4},{5,7},{7,5},{8,10},{10,8},{9,1... | collective-permute-start | bytes 1572872 | tf_op jit(solution)/shard_map/sum_fc/ppermute | solution.py:45
  437.3 14.1 %collective-permute-start.34 = (bf16[128,512]{1,0:T(8,128)(2,1)}, bf16[128,512]{1,0:T(8,128)(2,1)S(1)}, u32[]{:S(2)}, u32[]{:S(2)}) collective-permute-start(bf16[128,512]{1,0:T(8,128)(2,1)} %get-tuple-element.138), channel_id=1, source_target_pairs={{0,8},{4,12},{8,0},{12,4},{16,24},{20,28},{24,16},{28,20},{1,9},{5... | collective-permute-start | bytes 393224 | tf_op jit(solution)/shard_map/sum_heads/ppermute | solution.py:45
  445.7 4.3 collective-permute-start.43
  445.7 36.4 %collective-permute-start.28 = (bf16[512,1024]{1,0:T(8,128)(2,1)}, bf16[512,1024]{1,0:T(8,128)(2,1)}, u32[]{:S(2)}, u32[]{:S(2)}) collective-permute-start(bf16[512,1024]{1,0:T(8,128)(2,1)} %get-tuple-element.167), channel_id=1, source_target_pairs={{0,1},{1,0},{2,3},{3,2},{4,5},{5,4},{6,7},{7,6},{8,9},{9,8},{10,11... | collective-permute-start | bytes 3145736 | tf_op jit(solution)/shard_map/finish/ppermute | solution.py:45
  447.0 22.2 %copy-start.10 = (f32[128,1024]{1,0:T(8,128)}, f32[128,1024]{1,0:T(8,128)S(1)}, u32[]{:S(2)}) copy-start(f32[128,1024]{1,0:T(8,128)S(1)} %convert_add_fusion.3.refs_2_) | copy-start | bytes 1572868
  450.0 17.8 %collective-permute-start.40 = (f32[128,1024]{1,0:T(8,128)S(1)}, f32[128,1024]{1,0:T(8,128)S(1)}, u32[]{:S(2)}, u32[]{:S(2)}) collective-permute-start(f32[128,1024]{1,0:T(8,128)S(1)} %convert_add_fusion.3.refs_2_), channel_id=1, source_target_pairs={{0,2},{2,0},{1,3},{3,1},{4,6},{6,4},{5,7},{7,5},{8,10},{10,8},{9,1... | collective-permute-start | bytes 1572872 | tf_op jit(solution)/shard_map/sum_fc/ppermute | solution.py:45
  451.5 14.7 %collective-permute-start.44 = (f32[13,1024]{1,0:T(8,128)S(1)}, f32[13,1024]{1,0:T(8,128)S(1)}, u32[]{:S(2)}, u32[]{:S(2)}) collective-permute-start(f32[13,1024]{1,0:T(8,128)S(1)} %add.251), channel_id=1, source_target_pairs={{0,2},{2,0},{1,3},{3,1},{4,6},{6,4},{5,7},{7,5},{8,10},{10,8},{9,1... | collective-permute-start | bytes 159752 | tf_op jit(solution)/shard_map/vector_grads/ppermute | solution.py:45
  453.1 23.1 %copy-start.12 = (f32[128,512]{1,0:T(8,128)}, f32[128,512]{1,0:T(8,128)S(1)}, u32[]{:S(2)}) copy-start(f32[128,512]{1,0:T(8,128)S(1)} %convert_add_fusion.5.refs_2_) | copy-start | bytes 786436
  453.1 14.6 %copy-start.17 = (f32[128,1024]{1,0:T(8,128)}, f32[128,1024]{1,0:T(8,128)S(1)}, u32[]{:S(2)}) copy-start(f32[128,1024]{1,0:T(8,128)S(1)} %collective-permute-done.36.refs_1_) | copy-start | bytes 1572868
  453.1 23.1 %collective-permute-start.30 = (f32[128,512]{1,0:T(8,128)S(1)}, f32[128,512]{1,0:T(8,128)S(1)}, u32[]{:S(2)}, u32[]{:S(2)}) collective-permute-start(f32[128,512]{1,0:T(8,128)S(1)} %convert_add_fusion.6.refs_0_), channel_id=1, source_target_pairs={{0,2},{2,0},{1,3},{3,1},{4,6},{6,4},{5,7},{7,5},{8,10},{10,8},{9,1... | collective-permute-start | bytes 786440 | tf_op jit(solution)/shard_map/sum_heads/ppermute | solution.py:45
  466.2 10.0 %collective-permute-start.35 = (f32[128,512]{1,0:T(8,128)S(1)}, f32[128,512]{1,0:T(8,128)}, u32[]{:S(2)}, u32[]{:S(2)}) collective-permute-start(f32[128,512]{1,0:T(8,128)S(1)} %convert_add_fusion.5.refs_2_), channel_id=1, source_target_pairs={{0,2},{2,0},{1,3},{3,1},{4,6},{6,4},{5,7},{7,5},{8,10},{10,8},{9,1... | collective-permute-start | bytes 786440 | tf_op jit(solution)/shard_map/sum_heads/ppermute | solution.py:45
  468.6 12.9 %collective-permute-start.45 = (f32[13,1024]{1,0:T(8,128)S(1)}, f32[13,1024]{1,0:T(8,128)S(1)}, u32[]{:S(2)}, u32[]{:S(2)}) collective-permute-start(f32[13,1024]{1,0:T(8,128)S(1)} %add.252), channel_id=1, source_target_pairs={{0,16},{4,20},{8,24},{12,28},{16,0},{20,4},{24,8},{28,12},{1,17},{... | collective-permute-start | bytes 159752 | tf_op jit(solution)/shard_map/vector_grads/ppermute | solution.py:45
  (18 other events, 79.1 us)
